TPU v7x, 256 devices: a whole 4x4x8 slice. The times are simulated.
256 devices in a mesh: ctx: 64 (over x, z, core), head: 4 (over y).
Axes of the slice: x: 4, y: 4, z: 8, core: 2. Of those that a mesh axis runs over, the one named last changes fastest.
Arguments:
- hidden: bfloat16 [65536, 1536], P('ctx', 'head'), may hold values from -6 to 6
- norm_gain: float32 [1536], replicated, may hold values from 0.1 to 1.9
- zx_weight: bfloat16 [1536, 2, 3072], P(None, None, 'head'), may hold values from -0.15625 to 0.15625
- bc_weight: bfloat16 [1536, 256], replicated, may hold values from -0.15625 to 0.15625
- dt_weight: bfloat16 [1536, 48], P(None, 'head'), may hold values from -0.15625 to 0.15625
- conv_x: float32 [5, 3072], P(None, 'head'), may hold values from -0.5 to 0.5
- conv_bc: float32 [5, 256], replicated, may hold values from -0.5 to 0.5
- dt_bias: float32 [48], P('head'), may hold values from -4.6 to -2.3
- log_decay: float32 [65536, 48], P('ctx', 'head'), may hold values from -1.5 to 0, as said below
- skip_gain: float32 [48], P('head'), may hold values from 0.5 to 2
- out_gain: float32 [3072], P('head'), may hold values from 0.1 to 1.9
- out_weight: bfloat16 [3072, 1536], P('head'), may hold values from -0.109375 to 0.109375
Outputs:
- mixed: bfloat16 [65536, 1536], P('ctx', 'head')
Inputs may be any that keep to these rules, and one draw needn't show every extreme that they name: `log_decay`: negative everywhere; in some heads a token keeps only a few percent of the state after a few tens of positions, other heads decay over the whole document, and a head may lose a sizeable share of its state at single tokens.
All inputs are finite; a program needn't handle non-finite values.
Results may differ from a plain program's by a relative error of at most 0.015.
Values may be sent and summed in bfloat16 or wider, within the bound.
No kernel may reach another device: no remote copies, remote signals or barrier semaphores. Data moves between devices by JAX's collectives and lax.ppermute only.
A program may use at most 128 MiB of HBM per device.

v0:
```python
import functools
import jax
import jax.numpy as jnp
from jax import lax
from jax.experimental import pallas as pl
from jax.experimental.pallas import tpu as pltpu
from jax.sharding import PartitionSpec as P

HEADDIM = 64
STATE = 128
CONV = 4
BLOCK = 256
INNER = 3072
D = 1536
LANES = 128
RIM = 16
VMEM = 24 * 2**20
LIGHT = pl.CostEstimate(flops=1024, bytes_accessed=1024, transcendentals=0)
eps = 1e-05
f32 = jnp.float32
bf16 = jnp.bfloat16


def kept(*arrays):
    return [pltpu.with_memory_space_constraint(v, pltpu.HBM) for v in arrays]


def far_memory(shape, kind):
    return pltpu.HBM(shape, kind)


def split(v):
    hi = v.astype(bf16)
    return jnp.concatenate([hi, (v - hi.astype(f32)).astype(bf16)], axis=1)


def coded(v):
    hi = v.astype(bf16).astype(f32)
    return jnp.concatenate([hi, v - hi], axis=0).astype(bf16)


def decoded(v):
    wide = v.astype(f32)
    return wide[:8] + wide[8:]


def silu(v):
    return 0.5 * v * (1.0 + jnp.tanh(0.5 * v))


def prepare_kernel(
    heads, inner, blocks,
    log_decay_t, dt_t, bc_weight, conv_x, conv_bc, dt_bias, skip_gain,
    decay, decay_t, to_end, channels, total, spread, thrice, others, taps, bias,
):
    lower = lax.broadcasted_iota(jnp.int32, (BLOCK, BLOCK), 0)
    upper = lax.broadcasted_iota(jnp.int32, (BLOCK, BLOCK), 1)
    ones = (lower <= upper).astype(f32)
    highest = lax.Precision.HIGHEST

    def dot(u, v):
        return jnp.dot(u, v, preferred_element_type=f32, precision=highest)

    def tall(v):
        padded = jnp.concatenate([v, jnp.zeros((LANES - heads, v.shape[1]), f32)], axis=0)
        return jnp.transpose(padded)

    lanes = lax.broadcasted_iota(jnp.int32, (LANES, inner), 0)
    head_of = lax.broadcasted_iota(jnp.int32, (LANES, inner), 1) // HEADDIM
    one_hot = (lanes == head_of).astype(f32)
    spread[0:LANES] = one_hot.astype(bf16)
    spread[LANES:] = one_hot.astype(bf16)
    three = (lanes == head_of) | (lanes == head_of + heads) | (lanes == head_of + 2 * heads)
    thrice[...] = three.astype(f32).astype(bf16)
    decay_t[...] = jnp.zeros_like(decay_t)
    totals = []
    for k in range(blocks):
        span = slice(k * BLOCK, (k + 1) * BLOCK)
        sums_t = dot(log_decay_t[:, span], ones)
        decay_t[0:heads, span] = sums_t
        sums = tall(sums_t)
        decay[span] = sums
        last = sums[BLOCK - 1 : BLOCK]
        to_end[span] = jnp.exp(last - sums)
        totals.append(last)
    rows = [jnp.exp(v) for v in totals]
    fades = []
    for h in range(2):
        passed = jnp.zeros((1, LANES), f32)
        for k in range(blocks // 2):
            rows.append(jnp.exp(passed))
            passed = passed + totals[h * (blocks // 2) + k]
        fades.append(passed)
    rows += [jnp.exp(v) for v in fades]

    def row(v):
        return jnp.concatenate([v, jnp.zeros((1, LANES - heads), f32)], axis=1)

    rows.append(row(skip_gain[...]))
    rows.append(jnp.ones((1, LANES), f32))
    while len(rows) < 16:
        rows.append(jnp.zeros((1, LANES), f32))
    channels[...] = dot(jnp.concatenate(rows, axis=0), one_hot)
    whole = fades[0] + fades[1]
    high = whole.astype(bf16).astype(f32)
    mid = (whole - high).astype(bf16).astype(f32)
    low = whole - high - mid
    total[...] = jnp.concatenate(
        [high[:, :heads], mid[:, :heads], low[:, :heads], jnp.zeros((1, LANES - 3 * heads), f32)], axis=1
    )
    bias[...] = row(dt_bias[...])
    others[:, : 2 * STATE] = bc_weight[...]
    others[:, 2 * STATE :] = tall(dt_t[...].astype(f32)).astype(bf16)
    taps[0 : CONV + 1, :inner] = conv_x[...]
    taps[0 : CONV + 1, inner:] = conv_bc[...]


def prepare(log_decay_t, dt_t, bc_weight, conv_x, conv_bc, dt_bias, skip_gain):
    heads, rows = log_decay_t.shape
    inner = conv_x.shape[1]
    blocks = rows // BLOCK
    shapes = [
        ((rows, LANES), f32), ((16, rows), f32), ((rows, LANES), f32), ((16, inner), f32),
        ((1, LANES), f32), ((2 * LANES, inner), bf16), ((LANES, inner), bf16),
        ((D, 2 * STATE + LANES), bf16), ((CONV + 1, inner + 2 * STATE), f32), ((1, LANES), f32),
    ]
    return pl.pallas_call(
        functools.partial(prepare_kernel, heads, inner, blocks),
        out_shape=[jax.ShapeDtypeStruct(*v) for v in shapes],
        compiler_params=pltpu.CompilerParams(vmem_limit_bytes=VMEM),
        cost_estimate=LIGHT,
        name="prepare",
    )(log_decay_t, dt_t, bc_weight, conv_x, conv_bc, dt_bias, skip_gain)


def gather_kernel(
    owners, own, from_left, from_right, gain_0, gain_1, gain_2, w_0, w_1, w_2, o_0, o_1, o_2,
    acc, acc_others, squares, lhs,
):
    width = own.shape[1]
    step = pl.program_id(0)

    @pl.when(step == 0)
    def _():
        square = None
        for k, (piece, gain) in enumerate(((own, gain_0), (from_left, gain_1), (from_right, gain_2))):
            values = piece[...].astype(f32)
            lhs[:, k * width : (k + 1) * width] = (values * gain[0]).astype(bf16)
            part = jnp.sum(values * values, axis=1, keepdims=True)
            square = part if square is None else square + part
        squares[...] = square

    acc[0] = jnp.dot(
        lhs[...], jnp.concatenate([w_0[0], w_1[0], w_2[0]], axis=0), preferred_element_type=f32
    )

    @pl.when(step == 1)
    def _():
        acc_others[...] = jnp.dot(
            lhs[...], jnp.concatenate([o_0[...], o_1[...], o_2[...]], axis=0),
            preferred_element_type=f32,
        )


def gather(owners, own, from_left, from_right, gains, gate_x, others):
    rows, width = own.shape
    inner = gate_x.shape[2]
    narrow = others.shape[1]

    def whole(*shape):
        return pl.BlockSpec(shape, lambda n, o: (0,) * len(shape))

    def gain(k):
        return pl.BlockSpec((1, 1, width), lambda n, o: (o[k], 0, 0))

    def wide(k):
        return pl.BlockSpec((1, width, inner), lambda n, o: (n, o[k], 0))

    def small(k):
        return pl.BlockSpec((width, narrow), lambda n, o: (o[k], 0))

    return pl.pallas_call(
        gather_kernel,
        grid_spec=pltpu.PrefetchScalarGridSpec(
            num_scalar_prefetch=1,
            grid=(2,),
            in_specs=[whole(rows, width)] * 3 + [f(k) for f in (gain, wide, small) for k in range(3)],
            out_specs=[
                pl.BlockSpec((1, rows, inner), lambda n, o: (n, 0, 0)), whole(rows, narrow), whole(rows, 1),
            ],
            scratch_shapes=[pltpu.VMEM((rows, 3 * width), bf16)],
        ),
        out_shape=[
            far_memory((2, rows, inner), f32), far_memory((rows, narrow), f32), far_memory((rows, 1), f32),
        ],
        compiler_params=pltpu.CompilerParams(vmem_limit_bytes=VMEM),
        cost_estimate=LIGHT,
        name="gather",
    )(owners, own, from_left, from_right, gains, gains, gains, gate_x, gate_x, gate_x, others, others, others)


def front_kernel(
    inner, last,
    owner, acc, acc_others, piece, squares, gain, gate_x, others, near, taps, dt_bias, to_end, spread, keep, total,
    *rest,
):
    if last:
        later, join, gate, x_out, bc_out, xs_out, entering, state, payload, extended, slabs = rest
    else:
        rim_acc, rim_others, rim_piece, rim_squares, gate, x_out, bc_out, xs_out, entering, state, tail, extended = rest
    index = pl.program_id(0)
    wide = inner + 2 * STATE

    def scaled(piece):
        values = piece[...].astype(f32)
        return values, (values * gain[0]).astype(bf16)

    def row_scale(squares, values):
        square = squares[...] + jnp.sum(values * values, axis=1, keepdims=True)
        return lax.rsqrt(square * (1.0 / D) + eps)

    def dot(u, v):
        return jnp.dot(u, v, preferred_element_type=f32)

    @pl.when(index == 0)
    def _():
        state[...] = jnp.zeros_like(state)
        if last:
            extended[0:RIM] = near[...].astype(f32)
        else:
            values, lhs = scaled(rim_piece)
            scale = row_scale(rim_squares, values)
            x_rim = (rim_acc[1] + dot(lhs, gate_x[1])) * scale
            bc_rim = (
                rim_others[:, : 2 * STATE] + dot(lhs, others[:, : 2 * STATE])
            ) * scale
            extended[0:RIM, :inner] = x_rim.astype(bf16).astype(f32)
            extended[0:RIM, inner:] = bc_rim.astype(bf16).astype(f32)

    @pl.when(index > 0)
    def _():
        extended[0:RIM] = extended[BLOCK : BLOCK + RIM]

    values, lhs = scaled(piece)
    scale = row_scale(squares, values)
    gate[...] = ((acc[0] + dot(lhs, gate_x[0])) * scale).astype(bf16)
    x_raw = ((acc[1] + dot(lhs, gate_x[1])) * scale).astype(bf16)
    others_raw = ((acc_others[...] + dot(lhs, others[...])) * scale).astype(bf16)
    extended[RIM : RIM + BLOCK, :inner] = x_raw.astype(f32)
    extended[RIM : RIM + BLOCK, inner:] = others_raw[:, : 2 * STATE].astype(f32)
    step = jax.nn.softplus(others_raw[:, 2 * STATE :].astype(f32) + dt_bias[...])
    summed = taps[CONV : CONV + 1]
    for k in range(CONV):
        first = RIM - CONV + 1 + k
        summed = summed + taps[k : k + 1] * extended[first : first + BLOCK]
    conv = silu(summed)
    x_conv = conv[:, :inner].astype(bf16)
    bc = conv[:, inner:].astype(bf16)
    x_out[...] = x_conv
    bc_out[...] = bc
    x_wide = x_conv.astype(f32)
    by_step = dot(split(step), spread[...])
    by_end = dot(split(step * to_end[...]), spread[...])
    xs_out[...] = (x_wide * by_step).astype(bf16)
    weighted = (x_wide * by_end).astype(bf16)
    entering[0] = state[...]
    state[...] = keep[0] * state[...] + lax.dot_general(
        bc[:, :STATE], weighted, (((0,), (0,)), ((), ())), preferred_element_type=f32
    )

    @pl.when(index == pl.num_programs(0) - 1)
    def _():
        if last:
            half = STATE // 2
            chunks = inner // LANES
            joined = join[0] * state[...] + later[...]
            slabs[...] = jnp.zeros_like(slabs)
            for c in range(chunks):
                slabs[:, c] = joined[0:half, c * LANES : (c + 1) * LANES]
                slabs[:, chunks + c] = joined[half:STATE, c * LANES : (c + 1) * LANES]
            slabs[:, 2 * chunks] = jnp.broadcast_to(total[...], (half, LANES))
            payload[...] = slabs[...].astype(bf16)
        else:
            tail[...] = extended[BLOCK : BLOCK + RIM].astype(bf16)


def front(
    last, half, owner, acc, acc_others, piece, squares, gains, gate_x, others, near, taps, dt_bias, to_end,
    spread, keep, total, *more,
):
    width = piece.shape[1]
    inner = gate_x.shape[2]
    grid = to_end.shape[0] // BLOCK // 2
    rows = grid * BLOCK
    base = half * grid
    wide = inner + 2 * STATE
    pieces = STATE // 2

    def row(width, offset=0):
        return pl.BlockSpec((BLOCK, width), lambda i, o: (i + offset, 0))

    def whole(*shape):
        return pl.BlockSpec(shape, lambda i, o: (0,) * len(shape))

    def rim(width):
        return pl.BlockSpec((RIM, width), lambda i, o: (rows // RIM, 0))

    if last:
        operands = more
        extra = [whole(STATE, inner), pl.BlockSpec((1, 1, inner), lambda i, o: (9, 0, 0))]
        out_spec, out_shape = whole(pieces, 16, LANES), (pieces, 16, LANES)
        scratch = [pltpu.VMEM((pieces, 16, LANES), f32)]
    else:
        operands = (acc, acc_others, piece, squares)
        extra = [
            pl.BlockSpec((2, RIM, inner), lambda i, o: (0, rows // RIM, 0)),
            rim(acc_others.shape[1]), rim(width), rim(1),
        ]
        out_spec, out_shape = whole(RIM, wide), (RIM, wide)
        scratch = []
    return pl.pallas_call(
        functools.partial(front_kernel, inner, last),
        grid_spec=pltpu.PrefetchScalarGridSpec(
            num_scalar_prefetch=1,
            grid=(grid,),
            in_specs=[
                pl.BlockSpec((2, BLOCK, inner), lambda i, o: (0, i, 0)), row(acc_others.shape[1]),
                row(width), row(1),
                pl.BlockSpec((1, 1, width), lambda i, o: (o[0], 0, 0)),
                pl.BlockSpec((2, width, inner), lambda i, o: (0, o[0], 0)),
                pl.BlockSpec((width, others.shape[1]), lambda i, o: (o[0], 0)),
                whole(RIM, wide), whole(CONV + 1, wide),
                whole(1, LANES), row(LANES, base), whole(2 * LANES, inner),
                pl.BlockSpec((1, 1, inner), lambda i, o: (i + base, 0, 0)), whole(1, LANES),
            ] + extra,
            out_specs=[
                row(inner), row(inner), row(2 * STATE), row(inner),
                pl.BlockSpec((1, STATE, inner), lambda i, o: (i, 0, 0)),
                whole(STATE, inner), out_spec,
            ],
            scratch_shapes=[pltpu.VMEM((BLOCK + RIM, wide), f32)] + scratch,
        ),
        out_shape=[
            far_memory((rows, inner), bf16),
            far_memory((rows, inner), bf16),
            far_memory((rows, 2 * STATE), bf16),
            far_memory((rows, inner), bf16),
            far_memory((grid, STATE, inner), f32),
            jax.ShapeDtypeStruct((STATE, inner), f32),
            jax.ShapeDtypeStruct(out_shape, bf16),
        ],
        compiler_params=pltpu.CompilerParams(vmem_limit_bytes=VMEM),
        cost_estimate=LIGHT,
        name="front",
    )(owner, acc, acc_others, piece, squares, gains, gate_x, others, near, taps, dt_bias, to_end, spread, keep, total, *operands)


def scan_kernel(chunks, taken, spread, given, decays, sums):
    count = taken.shape[0]
    wide = taken[...].astype(f32)
    decays[...] = wide
    rows = decays[:, 2 * chunks]
    gains = jnp.exp(jnp.dot(rows.astype(bf16), spread[...], preferred_element_type=f32))
    sums[...] = wide
    decays[...] = jnp.zeros_like(decays)
    for c in range(chunks):
        part = gains[:, c * LANES : (c + 1) * LANES]
        decays[:, c] = part
        decays[:, chunks + c] = part
    running = jnp.zeros(taken.shape[1:], f32)
    for j in range(count):
        following = decays[j] * running + sums[j]
        sums[j] = running
        running = following
    given[...] = sums[...].astype(bf16)


def scan(taken, spread):
    chunks = spread.shape[1] // LANES
    return pl.pallas_call(
        functools.partial(scan_kernel, chunks),
        out_shape=jax.ShapeDtypeStruct(taken.shape, bf16),
        scratch_shapes=[pltpu.VMEM(taken.shape, f32), pltpu.VMEM(taken.shape, f32)],
        name="scan",
    )(taken, spread)


def inside_kernel(heads, bc, xs, decay, decay_t, out):
    both = bc[...]
    scores = lax.dot_general(
        both[:, STATE:], both[:, :STATE], (((1,), (1,)), ((), ())), preferred_element_type=f32
    )
    row = lax.broadcasted_iota(jnp.int32, (BLOCK, BLOCK), 0)
    column = lax.broadcasted_iota(jnp.int32, (BLOCK, BLOCK), 1)
    scores = jnp.where(row >= column, scores, 0.0)
    sums = decay[...]
    first = lax.broadcasted_iota(jnp.int32, (BLOCK, LANES), 1) < HEADDIM
    for pair in range(heads // 2):
        span = slice(pair * LANES, (pair + 1) * LANES)
        found = []
        for h in (2 * pair, 2 * pair + 1):
            gap = jnp.minimum(sums[:, h : h + 1] - decay_t[h : h + 1, :], 0.0)
            mix = (scores * jnp.exp(gap)).astype(bf16)
            found.append(jnp.dot(mix, xs[:, span], preferred_element_type=f32))
        out[:, span] = jnp.where(first, found[0], found[1])


def inside(bc, xs, decay, decay_t, half):
    rows, inner = xs.shape
    grid = rows // BLOCK
    base = half * grid
    return pl.pallas_call(
        functools.partial(inside_kernel, inner // HEADDIM),
        grid=(grid,),
        in_specs=[
            pl.BlockSpec((BLOCK, 2 * STATE), lambda i: (i, 0)),
            pl.BlockSpec((BLOCK, inner), lambda i: (i, 0)),
            pl.BlockSpec((BLOCK, LANES), lambda i: (i + base, 0)),
            pl.BlockSpec((16, BLOCK), lambda i: (0, i + base)),
        ],
        out_specs=pl.BlockSpec((BLOCK, inner), lambda i: (i, 0)),
        out_shape=far_memory((rows, inner), f32),
        compiler_params=pltpu.CompilerParams(vmem_limit_bytes=VMEM),
        cost_estimate=LIGHT,
        name="inside",
    )(bc, xs, decay, decay_t)


def tail_kernel(
    inner, half_index,
    y_in, x_conv, gate, bc, entering, taken, earlier, fade_in, before, skip, decay, spread, gain, weight,
    far, right, left, own, squares, slabs, incoming,
):
    chunks = inner // LANES

    @pl.when(pl.program_id(0) == 0)
    def _():
        squares[...] = jnp.zeros_like(squares)
        slabs[...] = taken[...].astype(f32)
        half = STATE // 2
        for c in range(chunks):
            incoming[0:half, c * LANES : (c + 1) * LANES] = slabs[:, c]
            incoming[half:STATE, c * LANES : (c + 1) * LANES] = slabs[:, chunks + c]
        if half_index:
            incoming[...] = earlier[...] + fade_in[0] * incoming[...]

    carried = (entering[0] + before[0] * incoming[...]).astype(bf16)
    fade = jnp.dot(split(jnp.exp(decay[...])), spread[...], preferred_element_type=f32)
    y = y_in[...] + fade * jnp.dot(bc[:, STATE:], carried, preferred_element_type=f32)
    y = y + skip[0] * x_conv[...].astype(f32)
    gated = y * silu(gate[...].astype(f32))
    step = pl.program_id(0)
    square = jnp.sum(gated * gated, axis=1, keepdims=True)
    squares[pl.ds(step, 1)] = jnp.transpose(jnp.broadcast_to(square, (BLOCK, LANES)))[:1]
    scaled = (gated * gain[...]).astype(bf16)
    width = far.shape[1]
    place = pl.ds(pl.multiple_of(step * BLOCK, BLOCK), BLOCK)
    outs = (own, right, far, left)
    for n, out in enumerate(outs):
        out[place] = jnp.dot(
            scaled, weight[:, n * width : (n + 1) * width], preferred_element_type=f32
        ).astype(bf16)

    @pl.when(step == pl.num_programs(0) - 1)
    def _():
        rows = far.shape[0] - 16
        parts = coded(squares[...])
        for out in outs:
            out[rows : rows + 16, :BLOCK] = parts
            out[rows : rows + 16, BLOCK:] = jnp.zeros((16, width - BLOCK), bf16)


def tail(half, y_in, x_conv, gate, bc, entering, taken, earlier, channels, decay, spread, gain, weight):
    rows, inner = y_in.shape
    grid = rows // BLOCK
    base = half * grid
    blocks = 2 * grid

    def channel(first, stride=0):
        return pl.BlockSpec((1, 1, inner), lambda i: (first + stride * i, 0, 0))

    width = weight.shape[1] // 4

    def row(width, offset=0):
        return pl.BlockSpec((BLOCK, width), lambda i: (i + offset, 0))

    def whole(*shape):
        return pl.BlockSpec(shape, lambda i: (0,) * len(shape))

    return pl.pallas_call(
        functools.partial(tail_kernel, inner, half),
        grid=(grid,),
        in_specs=[
            row(inner), row(inner), row(inner), row(2 * STATE),
            pl.BlockSpec((1, STATE, inner), lambda i: (i, 0, 0)),
            whole(*taken.shape), whole(STATE, inner), channel(2 * blocks), channel(blocks + base, 1),
            channel(2 * blocks + 2), row(LANES, base), whole(2 * LANES, inner), whole(1, inner),
            whole(*weight.shape),
        ],
        out_specs=[whole(rows + 16, width)] * 4,
        out_shape=[far_memory((rows + 16, width), bf16)] * 4,
        scratch_shapes=[
            pltpu.VMEM((8, BLOCK), f32), pltpu.VMEM(taken.shape, f32), pltpu.VMEM((STATE, inner), f32),
        ],
        compiler_params=pltpu.CompilerParams(vmem_limit_bytes=VMEM),
        cost_estimate=LIGHT,
        name="tail",
    )(
        y_in, x_conv, gate, bc, entering, taken, earlier, channels, channels, channels, decay, spread, gain,
        weight,
    )


def add_kernel(u, v, out):
    rows = out.shape[0] - 16
    out[:rows] = (u[:rows].astype(f32) + v[:rows].astype(f32)).astype(bf16)
    out[rows:] = coded(decoded(u[rows:]) + decoded(v[rows:]))


def add(u, v):
    return pl.pallas_call(
        add_kernel, out_shape=jax.ShapeDtypeStruct(u.shape, bf16), cost_estimate=LIGHT, name="add"
    )(u, v)


def finish_kernel(own_a, direct_a, arrived_a, own_b, direct_b, arrived_b, out):
    rows = own_a.shape[0] - 16
    for h, parts in enumerate(((own_a, direct_a, arrived_a), (own_b, direct_b, arrived_b))):
        squares = sum(decoded(p[rows:, :BLOCK]) for p in parts)
        scales = jnp.transpose(lax.rsqrt(squares * (1.0 / INNER) + eps))
        for k in range(rows // BLOCK):
            span = slice(k * BLOCK, (k + 1) * BLOCK)
            total = sum(p[span].astype(f32) for p in parts)
            first = h * rows + k * BLOCK
            out[first : first + BLOCK] = (total * scales[:, k : k + 1]).astype(bf16)


def finish(*parts):
    rows, width = parts[0].shape
    return pl.pallas_call(
        finish_kernel, out_shape=jax.ShapeDtypeStruct((2 * (rows - 16), width), bf16),
        cost_estimate=LIGHT, name="finish",
    )(*parts)


def per_device(
    hidden, norm_gain, zx_weight, bc_weight, dt_weight, conv_x, conv_bc, dt_bias,
    log_decay, skip_gain, out_gain, out_weight,
):
    rows, width = hidden.shape
    heads = dt_weight.shape[1]
    inner = zx_weight.shape[2]
    blocks = rows // BLOCK
    middle = rows // 2
    groups = lax.axis_size("head")
    places = lax.axis_size("ctx")
    me = lax.axis_index("head")
    to_right = [(i, (i + 1) % groups) for i in range(groups)]
    to_left = [(i, (i - 1) % groups) for i in range(groups)]

    def right(v):
        return lax.ppermute(v, "head", to_right)

    def left(v):
        return lax.ppermute(v, "head", to_left)

    bottom = jnp.concatenate([hidden[middle:], hidden[middle - RIM : middle]], axis=0)
    right_bottom, left_bottom = right(bottom), left(bottom)
    gate_x = jnp.transpose(zx_weight, (1, 0, 2))
    gains = norm_gain.reshape(groups, 1, width)
    owners = jnp.stack([me, lax.rem(me + groups - 1, groups), lax.rem(me + 1, groups)]).astype(jnp.int32)
    owner = lax.rem(me + 2, groups).astype(jnp.int32)[None]
    right_bottom, hidden, gate_x, log_decay, dt_weight, bc_weight = lax.optimization_barrier(
        (right_bottom, hidden, gate_x, log_decay, dt_weight, bc_weight)
    )
    decay, decay_t, to_end, channels, total, spread, thrice, others, taps, bias = prepare(
        jnp.transpose(log_decay), jnp.transpose(dt_weight), bc_weight, conv_x, conv_bc,
        dt_bias[None], skip_gain[None],
    )
    gate_x, = kept(gate_x)
    far_bottom = right(right_bottom)
    top = hidden[:middle]
    left_top = left(top)
    acc_b, others_b, squares_b = gather(owners, bottom, right_bottom, left_bottom, gains, gate_x, others)
    left_top, acc_b, top = lax.optimization_barrier((left_top, acc_b, top))
    far_top = left(left_top)
    right_top = right(top)

    channels = channels[:, None]
    gain = out_gain[None]

    no_rim = jnp.zeros((RIM, inner + 2 * STATE), bf16)
    gate_b, x_b, bc_b, xs_b, enter_b, state_b, raw_tail = front(
        False, 1, owner, *kept(acc_b, others_b), far_bottom, *kept(squares_b), gains, gate_x, others, no_rim, taps,
        bias, to_end, spread, channels, total,
    )
    near = lax.ppermute(raw_tail, "ctx", [(i, i + 1) for i in range(places - 1)])
    acc_a, others_a, squares_a = gather(owners, top, right_top, left_top, gains, gate_x, others)
    gate_a, x_a, bc_a, xs_a, enter_a, state_a, payload = front(
        True, 0, owner, *kept(acc_a, others_a), far_top, *kept(squares_a), gains, gate_x, others, near, taps, bias,
        to_end, spread, channels, total, state_b, channels,
    )
    taken = lax.all_to_all(payload, "ctx", 0, 0)
    inside_a = inside(*kept(bc_a, xs_a), decay, decay_t, 0)
    turned = jnp.concatenate(
        [
            lax.dynamic_slice_in_dim(out_weight, lax.rem(me + k, groups) * width, width, 1)
            for k in range(groups)
        ],
        axis=1,
    )
    taken, inside_a, turned = lax.optimization_barrier((taken, inside_a, turned))
    incoming = lax.all_to_all(scan(taken, thrice), "ctx", 0, 0)
    inside_b = inside(*kept(bc_b, xs_b), decay, decay_t, 1)
    incoming, inside_b = lax.optimization_barrier((incoming, inside_b))

    far_a, right_a, left_a, own_a = tail(
        0, *kept(inside_a, x_a, gate_a, bc_a, enter_a), incoming, state_a, channels, decay, spread,
        gain, turned,
    )
    passed_a, direct_a = right(far_a), left(left_a)
    far_b, right_b, left_b, own_b = tail(
        1, *kept(inside_b, x_b, gate_b, bc_b, enter_b), incoming, *kept(state_a), channels, decay,
        spread, gain, turned,
    )
    passed_b, direct_b = left(far_b), right(right_b)
    arrived_a = right(add(right_a, passed_a))
    arrived_b = left(add(left_b, passed_b))
    return finish(own_a, direct_a, arrived_a, own_b, direct_b, arrived_b)


def solution(mesh):
    placed = (
        P("ctx", "head"), P(), P(None, None, "head"), P(), P(None, "head"), P(None, "head"), P(),
        P("head"), P("ctx", "head"), P("head"), P("head"), P("head", None),
    )
    return jax.shard_map(
        per_device, mesh=mesh, in_specs=placed, out_specs=P("ctx", "head"), check_vma=False
    )
```

profile of v0, /device:TPU:1, one launch (start us, length us, event | category | flops | bytes accessed | tf_op | source)
XLA Modules:
  0.0 150.3 jit_solution(3994985602398499520)
XLA Ops:
  0.0 0.7 slice.10
  0.7 1.0 slice.9
  1.8 0.0 copy-start.10
  1.8 0.0 copy-start.16
  1.8 0.0 copy-start.4
  1.8 0.0 copy-start.5
  1.8 0.0 copy-start.6
  1.9 0.0 copy-start.7
  1.9 0.0 copy-start.8
  1.9 0.0 copy-start.9
  1.9 2.2 %collective-permute-start = (bf16[528,384]{1,0:T(8,128)(2,1)S(1)}, bf16[528,384]{1,0:T(8,128)(2,1)}, u32[]{:S(2)}, u32[]{:S(2)}) collective-permute-start(bf16[528,384]{1,0:T(8,128)(2,1)S(1)} %pad_maximum_fusion.1.own), channel_id=1, source_target_pairs={{0,1},{1,2},{2,3},{3,0},{4,5},{5,6},{6,7},{7,4},{8,9},{9,10},{10,1... | collective-permute-start | bytes 1216520 | tf_op jit(solution)/shard_map/ppermute | solution.py:562
  4.1 1.5 %collective-permute-start.2 = (bf16[528,384]{1,0:T(8,128)(2,1)S(1)}, bf16[528,384]{1,0:T(8,128)(2,1)}, u32[]{:S(2)}, u32[]{:S(2)}) collective-permute-start(bf16[528,384]{1,0:T(8,128)(2,1)S(1)} %pad_maximum_fusion.1.own), channel_id=1, source_target_pairs={{0,3},{1,0},{2,1},{3,2},{4,7},{5,4},{6,5},{7,6},{8,11},{9,8},{10,9... | collective-permute-start | bytes 1216520 | tf_op jit(solution)/shard_map/ppermute | solution.py:565
  5.6 5.1 %copy.15 = bf16[1536,2,768]{2,0,1:T(8,128)(2,1)} copy(bf16[1536,2,768]{2,1,0:T(2,128)(2,1)} %param.14) | data formatting | bytes 9437184 | tf_op args[2]
  10.8 1.9 %collective-permute-done.from_left = bf16[528,384]{1,0:T(8,128)(2,1)} collective-permute-done((bf16[528,384]{1,0:T(8,128)(2,1)S(1)}, bf16[528,384]{1,0:T(8,128)(2,1)}, u32[]{:S(2)}, u32[]{:S(2)}) %collective-permute-start) | collective-permute-done | bytes 405536 | tf_op jit(solution)/shard_map/ppermute | solution.py:562
  12.7 0.8 slice.11.own
  13.5 3.2 %collective-permute-start.1 = (bf16[512,384]{1,0:T(8,128)(2,1)}, bf16[512,384]{1,0:T(8,128)(2,1)}, u32[]{:S(2)}, u32[]{:S(2)}) collective-permute-start(bf16[512,384]{1,0:T(8,128)(2,1)} %slice.11.own), channel_id=1, source_target_pairs={{0,3},{1,0},{2,1},{3,2},{4,7},{5,4},{6,5},{7,6},{8,11},{9,8},{10,9... | collective-permute-start | bytes 1179656 | tf_op jit(solution)/shard_map/ppermute | solution.py:565
  16.7 0.0 collective-permute-start.5
  16.7 0.1 pad_add_fusion.owners
  16.8 0.0 copy-start.2
  16.8 1.1 copy-done.2
  18.0 0.9 prepare.1
  18.9 0.7 copy-done.3
  19.6 0.0 collective-permute-done.2.from_right
  19.6 7.7 %gather.2 = (f32[2,528,768]{2,1,0:T(8,128)}, f32[528,384]{1,0:T(8,128)}, f32[528,1]{1,0:T(8,128)}) custom-call(s32[3]{0:T(128)S(1)} %pad_add_fusion.owners, bf16[528,384]{1,0:T(8,128)(2,1)S(1)} %pad_maximum_fusion.1.own, bf16[528,384]{1,0:T(8,128)(2,1)} %collective-permute-done.from_left, bf16[528,384]{1,0:T(8,128)(2,1)} %collective-permute-done.2.from_right, ...), custom_call_target="tpu_custom_call" | custom-call | flops 1024 | bytes 1024 | tf_op jit(solution)/shard_map/gather/pallas_call | solution.py:182
  27.3 0.0 collective-permute-done.1.from_right
  27.3 0.1 collective-permute-start.3
  27.4 2.7 %collective-permute-start.4 = (bf16[512,384]{1,0:T(8,128)(2,1)}, bf16[512,384]{1,0:T(8,128)(2,1)S(1)}, u32[]{:S(2)}, u32[]{:S(2)}) collective-permute-start(bf16[512,384]{1,0:T(8,128)(2,1)} %collective-permute-done.1.from_right), channel_id=1, source_target_pairs={{0,3},{1,0},{2,1},{3,2},{4,7},{5,4},{6,5},{7,6},{8,11},{9,8},{10,9... | collective-permute-start | bytes 1179656 | tf_op jit(solution)/shard_map/ppermute | solution.py:565
  30.2 8.4 %front.2 = (bf16[512,768]{1,0:T(8,128)(2,1)}, bf16[512,768]{1,0:T(8,128)(2,1)}, bf16[512,256]{1,0:T(8,128)(2,1)}, bf16[512,768]{1,0:T(8,128)(2,1)}, f32[2,128,76...) custom-call(s32[1]{0:T(128)} %bitcast.owner, f32[2,528,768]{2,1,0:T(8,128)} %get-tuple-element.70.acc.rest_0_, ...), custom_call_target="tpu_custom_call" | custom-call | flops 1024 | bytes 1024 | tf_op jit(solution)/shard_map/front/pallas_call | solution.py:321
  38.6 6.2 %collective-permute-start.6 = (bf16[16,1024]{1,0:T(8,128)(2,1)S(1)}, bf16[16,1024]{1,0:T(8,128)(2,1)S(1)}, u32[]{:S(2)}, u32[]{:S(2)}) collective-permute-start(bf16[16,1024]{1,0:T(8,128)(2,1)S(1)} %get-tuple-element.79), channel_id=1, source_target_pairs={{0,4},{4,8},{8,12},{12,16},{16,20},{20,24},{24,28},{28,32},{32,36}... | collective-permute-start | bytes 98312 | tf_op jit(solution)/shard_map/ppermute | solution.py:597
  44.7 0.0 collective-permute-done.3.from_left
  44.8 7.7 %gather.3 = (f32[2,512,768]{2,1,0:T(8,128)}, f32[512,384]{1,0:T(8,128)}, f32[512,1]{1,0:T(8,128)}) custom-call(s32[3]{0:T(128)S(1)} %pad_add_fusion.owners, bf16[512,384]{1,0:T(8,128)(2,1)} %slice.11.own, bf16[512,384]{1,0:T(8,128)(2,1)} %collective-permute-done.3.from_left, bf16[512,384]{1,0:T(8,128)(2,1)} %collective-permute-done.1.from_right, ...), custom_call_target="tpu_custom_call" | custom-call | flops 1024 | bytes 1024 | tf_op jit(solution)/shard_map/gather/pallas_call | solution.py:182
  52.5 0.0 collective-permute-done.4.piece
  52.5 8.6 %front.3 = (bf16[512,768]{1,0:T(8,128)(2,1)}, bf16[512,768]{1,0:T(8,128)(2,1)}, bf16[512,256]{1,0:T(8,128)(2,1)}, bf16[512,768]{1,0:T(8,128)(2,1)}, f32[2,128,76...) custom-call(s32[1]{0:T(128)} %bitcast.owner, f32[2,512,768]{2,1,0:T(8,128)} %get-tuple-element.67.acc, ...), custom_call_target="tpu_custom_call" | custom-call | flops 1024 | bytes 1024 | tf_op jit(solution)/shard_map/front/pallas_call | solution.py:321
  61.0 0.7 copy-done
  61.8 10.9 %all-to-all-start = ((bf16[64,16,128]{2,1,0:T(8,128)(2,1)}), bf16[64,16,128]{2,1,0:T(8,128)(2,1)}, u32[]{:S(2)}, u32[]{:S(2)}) async-start(bf16[64,16,128]{2,1,0:T(8,128)(2,1)} %get-tuple-element.81), calls=%async_computation | async-start | bytes 524288 | tf_op jit(solution)/shard_map/all_to_all | solution.py:603
  72.7 1.9 %constant_dynamic-slice_fusion.3 = (bf16[768,384]{1,0:T(8,128)(2,1)S(1)}, bf16[768,384]{1,0:T(8,128)(2,1)S(1)}, bf16[768,384]{1,0:T(8,128)(2,1)S(1)}, bf16[768,384]{1,0:T(8,128)(2,1)S(1)}) fusion(bf16[768,1536]{1,0:T(8,128)(2,1)} %param.23, s32[]{:T(128)S(6)} %select_n.12, s32[]{:T(128)S(6)} %select_n.13, s32[]{:T(128)S(6)} %select_n.15, s32[]{:T(128)S(6)} %select_n.14), kind=kLoop, calls=%fused_computation.6 | loop fusion | bytes 4718608 | tf_op jit(solution)/shard_map/dynamic_slice | solution.py:607
  74.6 0.2 pad_maximum_fusion.weight
  74.8 0.0 copy-start.17
  74.8 3.9 %inside.2.y_in = f32[512,768]{1,0:T(8,128)} custom-call(bf16[512,256]{1,0:T(8,128)(2,1)} %get-tuple-element.82.bc, bf16[512,768]{1,0:T(8,128)(2,1)} %get-tuple-element.83.xs, f32[1024,128]{1,0:T(8,128)S(1)} %get-tuple-element.84.decay, f32[16,1024]{1,0:T(8,128)S(1)} %get-tuple-element.85.decay_t), custom_call_target="tpu_custom_call" | custom-call | flops 1024 | bytes 1024 | tf_op jit(solution)/shard_map/inside/pallas_call | solution.py:412
  78.7 5.9 %all-to-all-done.taken = bf16[64,16,128]{2,1,0:T(8,128)(2,1)} async-done(((bf16[64,16,128]{2,1,0:T(8,128)(2,1)}), bf16[64,16,128]{2,1,0:T(8,128)(2,1)}, u32[]{:S(2)}, u32[]{:S(2)}) %all-to-all-start) | async-done | bytes 262176 | tf_op jit(solution)/shard_map/all_to_all | solution.py:603
  84.6 2.2 %scan.1 = bf16[64,16,128]{2,1,0:T(8,128)(2,1)} custom-call(bf16[64,16,128]{2,1,0:T(8,128)(2,1)} %all-to-all-done.taken, bf16[128,768]{1,0:T(8,128)(2,1)} %copy-done.3), custom_call_target="tpu_custom_call" | custom-call | tf_op jit(solution)/shard_map/scan/pallas_call | solution.py:380
  86.8 6.2 %all-to-all-start.1 = ((bf16[64,16,128]{2,1,0:T(8,128)(2,1)}), bf16[64,16,128]{2,1,0:T(8,128)(2,1)}, u32[]{:S(2)}, u32[]{:S(2)}) async-start(bf16[64,16,128]{2,1,0:T(8,128)(2,1)} %scan.1), calls=%async_computation.1 | async-start | bytes 524288 | tf_op jit(solution)/shard_map/all_to_all | solution.py:613
  93.0 3.9 %inside.3.y_in = f32[512,768]{1,0:T(8,128)} custom-call(bf16[512,256]{1,0:T(8,128)(2,1)} %get-tuple-element.92.bc, bf16[512,768]{1,0:T(8,128)(2,1)} %get-tuple-element.93.xs, f32[1024,128]{1,0:T(8,128)S(1)} %get-tuple-element.84.decay, f32[16,1024]{1,0:T(8,128)S(1)} %get-tuple-element.85.decay_t), custom_call_target="tpu_custom_call" | custom-call | flops 1024 | bytes 1024 | tf_op jit(solution)/shard_map/inside/pallas_call | solution.py:412
  96.9 8.0 %all-to-all-done.1.taken = bf16[64,16,128]{2,1,0:T(8,128)(2,1)} async-done(((bf16[64,16,128]{2,1,0:T(8,128)(2,1)}), bf16[64,16,128]{2,1,0:T(8,128)(2,1)}, u32[]{:S(2)}, u32[]{:S(2)}) %all-to-all-start.1) | async-done | bytes 262176 | tf_op jit(solution)/shard_map/all_to_all | solution.py:613
  104.9 1.0 copy-done.1
  105.9 6.0 %tail.2 = (bf16[528,384]{1,0:T(8,128)(2,1)}, bf16[528,384]{1,0:T(8,128)(2,1)}, bf16[528,384]{1,0:T(8,128)(2,1)}, bf16[528,384]{1,0:T(8,128)(2,1)}) custom-call(f32[512,768]{1,0:T(8,128)} %inside.2.y_in, bf16[512,768]{1,0:T(8,128)(2,1)} %get-tuple-element.87.x_conv, bf16[512,768]{1,0:T(8,128)(2,1)} %get-tuple-element.88.gate, ...), custom_call_target="tpu_custom_call" | custom-call | flops 1024 | bytes 1024 | tf_op jit(solution)/shard_map/tail/pallas_call | solution.py:490
  112.0 0.0 collective-permute-start.8
  112.0 6.3 %tail.3 = (bf16[528,384]{1,0:T(8,128)(2,1)}, bf16[528,384]{1,0:T(8,128)(2,1)}, bf16[528,384]{1,0:T(8,128)(2,1)}, bf16[528,384]{1,0:T(8,128)(2,1)}) custom-call(f32[512,768]{1,0:T(8,128)} %inside.3.y_in, bf16[512,768]{1,0:T(8,128)(2,1)} %get-tuple-element.102.x_conv, bf16[512,768]{1,0:T(8,128)(2,1)} %get-tuple-element.103.gate, ...), custom_call_target="tpu_custom_call" | custom-call | flops 1024 | bytes 1024 | tf_op jit(solution)/shard_map/tail/pallas_call | solution.py:490
  118.3 2.6 %collective-permute-start.11 = (bf16[528,384]{1,0:T(8,128)(2,1)}, bf16[528,384]{1,0:T(8,128)(2,1)S(1)}, u32[]{:S(2)}, u32[]{:S(2)}) collective-permute-start(bf16[528,384]{1,0:T(8,128)(2,1)} %get-tuple-element.108), channel_id=1, source_target_pairs={{0,3},{1,0},{2,1},{3,2},{4,7},{5,4},{6,5},{7,6},{8,11},{9,8},{10,9... | collective-permute-start | bytes 1216520 | tf_op jit(solution)/shard_map/ppermute | solution.py:565
  120.9 0.2 collective-permute-start.7
  121.2 1.2 collective-permute-start.10
  122.4 1.6 %collective-permute-done.8.v = bf16[528,384]{1,0:T(8,128)(2,1)} collective-permute-done((bf16[528,384]{1,0:T(8,128)(2,1)}, bf16[528,384]{1,0:T(8,128)(2,1)}, u32[]{:S(2)}, u32[]{:S(2)}) %collective-permute-start.8) | collective-permute-done | bytes 405536 | tf_op jit(solution)/shard_map/ppermute | solution.py:562
  124.0 2.0 %add.37 = bf16[528,384]{1,0:T(8,128)(2,1)} custom-call(bf16[528,384]{1,0:T(8,128)(2,1)} %get-tuple-element.99.u, bf16[528,384]{1,0:T(8,128)(2,1)} %collective-permute-done.8.v), custom_call_target="tpu_custom_call" | custom-call | flops 1024 | bytes 1024 | tf_op jit(solution)/shard_map/add/pallas_call | solution.py:521
  126.0 0.0 collective-permute-start.9
  126.0 3.2 %collective-permute-done.11.v = bf16[528,384]{1,0:T(8,128)(2,1)S(1)} collective-permute-done((bf16[528,384]{1,0:T(8,128)(2,1)}, bf16[528,384]{1,0:T(8,128)(2,1)S(1)}, u32[]{:S(2)}, u32[]{:S(2)}) %collective-permute-start.11) | collective-permute-done | bytes 405536 | tf_op jit(solution)/shard_map/ppermute | solution.py:565
  129.2 0.8 copy-done.15
  130.0 2.0 %add.38 = bf16[528,384]{1,0:T(8,128)(2,1)} custom-call(bf16[528,384]{1,0:T(8,128)(2,1)} %get-tuple-element.107.u, bf16[528,384]{1,0:T(8,128)(2,1)} %copy-done.15), custom_call_target="tpu_custom_call" | custom-call | flops 1024 | bytes 1024 | tf_op jit(solution)/shard_map/add/pallas_call | solution.py:521
  132.0 3.3 %collective-permute-start.12 = (bf16[528,384]{1,0:T(8,128)(2,1)}, bf16[528,384]{1,0:T(8,128)(2,1)S(1)}, u32[]{:S(2)}, u32[]{:S(2)}) collective-permute-start(bf16[528,384]{1,0:T(8,128)(2,1)} %add.38), channel_id=1, source_target_pairs={{0,3},{1,0},{2,1},{3,2},{4,7},{5,4},{6,5},{7,6},{8,11},{9,8},{10,9... | collective-permute-start | bytes 1216520 | tf_op jit(solution)/shard_map/ppermute | solution.py:565
  135.3 2.6 %collective-permute-done.7.direct_a = bf16[528,384]{1,0:T(8,128)(2,1)S(1)} collective-permute-done((bf16[528,384]{1,0:T(8,128)(2,1)}, bf16[528,384]{1,0:T(8,128)(2,1)S(1)}, u32[]{:S(2)}, u32[]{:S(2)}) %collective-permute-start.7) | collective-permute-done | bytes 405536 | tf_op jit(solution)/shard_map/ppermute | solution.py:565
  137.9 0.0 collective-permute-done.10.direct_b
  137.9 2.9 %collective-permute-done.9.arrived_a = bf16[528,384]{1,0:T(8,128)(2,1)S(1)} collective-permute-done((bf16[528,384]{1,0:T(8,128)(2,1)}, bf16[528,384]{1,0:T(8,128)(2,1)S(1)}, u32[]{:S(2)}, u32[]{:S(2)}) %collective-permute-start.9) | collective-permute-done | bytes 405536 | tf_op jit(solution)/shard_map/ppermute | solution.py:562
  140.8 5.8 %collective-permute-done.12.arrived_b = bf16[528,384]{1,0:T(8,128)(2,1)S(1)} collective-permute-done((bf16[528,384]{1,0:T(8,128)(2,1)}, bf16[528,384]{1,0:T(8,128)(2,1)S(1)}, u32[]{:S(2)}, u32[]{:S(2)}) %collective-permute-start.12) | collective-permute-done | bytes 405536 | tf_op jit(solution)/shard_map/ppermute | solution.py:565
  146.6 0.7 copy-done.14
  147.4 3.0 %finish.1 = bf16[1024,384]{1,0:T(8,128)(2,1)} custom-call(bf16[528,384]{1,0:T(8,128)(2,1)} %get-tuple-element.97.own_a, bf16[528,384]{1,0:T(8,128)(2,1)} %copy-done.11, bf16[528,384]{1,0:T(8,128)(2,1)} %copy-done.13, bf16[528,384]{1,0:T(8,128)(2,1)} %get-tuple-element.105.own_b, bf16[528,384]{1,0:T(8,128)(2,1)} %copy-done.12, bf16[528,384]{1,0:T(8,128)(2,1)} %copy-done.14), custom_call_target="tpu_custom_call" | custom-call | flops 1024 | bytes 1024 | tf_op jit(solution)/shard_map/finish/pallas_call | solution.py:540
  (27 shorter events, 0.1 us)
Async XLA Ops:
  1.8 10.9 %copy-start.10 = (bf16[1024,384]{1,0:T(8,128)(2,1)S(1)}, bf16[1024,384]{1,0:T(8,128)(2,1)}, u32[]{:S(2)}) copy-start(bf16[1024,384]{1,0:T(8,128)(2,1)} %param.12) | copy-start | bytes 2359300
  1.8 14.9 %copy-start.16 = (f32[1536]{0:T(1024)S(1)}, f32[1536]{0:T(1024)}, u32[]{:S(2)}) copy-start(f32[1536]{0:T(1024)} %param.13) | copy-start | bytes 18436
  1.8 14.9 %copy-start.4 = (f32[1024,12]{0,1:T(8,128)S(1)}, f32[1024,12]{0,1:T(8,128)}, u32[]{:S(2)}) copy-start(f32[1024,12]{0,1:T(8,128)} %param.20) | copy-start | bytes 147460
  1.8 14.9 %copy-start.5 = (bf16[1536,12]{0,1:T(8,128)(2,1)S(1)}, bf16[1536,12]{0,1:T(8,128)(2,1)}, u32[]{:S(2)}) copy-start(bf16[1536,12]{0,1:T(8,128)(2,1)} %param.16) | copy-start | bytes 110596
  1.8 14.9 %copy-start.6 = (f32[5,768]{1,0:T(8,128)S(1)}, f32[5,768]{1,0:T(8,128)}, u32[]{:S(2)}) copy-start(f32[5,768]{1,0:T(8,128)} %conv_x.1) | copy-start | bytes 46084
  1.9 14.9 %copy-start.7 = (f32[5,256]{1,0:T(8,128)S(1)}, f32[5,256]{1,0:T(8,128)}, u32[]{:S(2)}) copy-start(f32[5,256]{1,0:T(8,128)} %conv_bc.1) | copy-start | bytes 15364
  1.9 14.9 %copy-start.8 = (f32[12]{0:T(128)S(1)}, f32[12]{0:T(128)}, u32[]{:S(2)}) copy-start(f32[12]{0:T(128)} %param.19) | copy-start | bytes 148
  1.9 14.9 %copy-start.9 = (f32[12]{0:T(128)S(1)}, f32[12]{0:T(128)}, u32[]{:S(2)}) copy-start(f32[12]{0:T(128)} %param.21) | copy-start | bytes 148
  1.9 10.8 %collective-permute-start = (bf16[528,384]{1,0:T(8,128)(2,1)S(1)}, bf16[528,384]{1,0:T(8,128)(2,1)}, u32[]{:S(2)}, u32[]{:S(2)}) collective-permute-start(bf16[528,384]{1,0:T(8,128)(2,1)S(1)} %pad_maximum_fusion.1.own), channel_id=1, source_target_pairs={{0,1},{1,2},{2,3},{3,0},{4,5},{5,6},{6,7},{7,4},{8,9},{9,10},{10,1... | collective-permute-start | bytes 1216520 | tf_op jit(solution)/shard_map/ppermute | solution.py:562
  4.1 15.5 %collective-permute-start.2 = (bf16[528,384]{1,0:T(8,128)(2,1)S(1)}, bf16[528,384]{1,0:T(8,128)(2,1)}, u32[]{:S(2)}, u32[]{:S(2)}) collective-permute-start(bf16[528,384]{1,0:T(8,128)(2,1)S(1)} %pad_maximum_fusion.1.own), channel_id=1, source_target_pairs={{0,3},{1,0},{2,1},{3,2},{4,7},{5,4},{6,5},{7,6},{8,11},{9,8},{10,9... | collective-permute-start | bytes 1216520 | tf_op jit(solution)/shard_map/ppermute | solution.py:565
  13.5 13.8 %collective-permute-start.1 = (bf16[512,384]{1,0:T(8,128)(2,1)}, bf16[512,384]{1,0:T(8,128)(2,1)}, u32[]{:S(2)}, u32[]{:S(2)}) collective-permute-start(bf16[512,384]{1,0:T(8,128)(2,1)} %slice.11.own), channel_id=1, source_target_pairs={{0,3},{1,0},{2,1},{3,2},{4,7},{5,4},{6,5},{7,6},{8,11},{9,8},{10,9... | collective-permute-start | bytes 1179656 | tf_op jit(solution)/shard_map/ppermute | solution.py:565
  16.7 13.5 %collective-permute-start.5 = (bf16[528,384]{1,0:T(8,128)(2,1)}, bf16[528,384]{1,0:T(8,128)(2,1)}, u32[]{:S(2)}, u32[]{:S(2)}) collective-permute-start(bf16[528,384]{1,0:T(8,128)(2,1)} %collective-permute-done.from_left), channel_id=1, source_target_pairs={{0,1},{1,2},{2,3},{3,0},{4,5},{5,6},{6,7},{7,4},{8,9},{9,10},{10,1... | collective-permute-start | bytes 1216520 | tf_op jit(solution)/shard_map/ppermute | solution.py:562
  16.8 1.1 copy-start.2
  18.9 0.7 copy-start.3
  27.3 17.5 %collective-permute-start.3 = (bf16[512,384]{1,0:T(8,128)(2,1)}, bf16[512,384]{1,0:T(8,128)(2,1)}, u32[]{:S(2)}, u32[]{:S(2)}) collective-permute-start(bf16[512,384]{1,0:T(8,128)(2,1)} %slice.11.own), channel_id=1, source_target_pairs={{0,1},{1,2},{2,3},{3,0},{4,5},{5,6},{6,7},{7,4},{8,9},{9,10},{10,1... | collective-permute-start | bytes 1179656 | tf_op jit(solution)/shard_map/ppermute | solution.py:562
  27.4 25.1 %collective-permute-start.4 = (bf16[512,384]{1,0:T(8,128)(2,1)}, bf16[512,384]{1,0:T(8,128)(2,1)S(1)}, u32[]{:S(2)}, u32[]{:S(2)}) collective-permute-start(bf16[512,384]{1,0:T(8,128)(2,1)} %collective-permute-done.1.from_right), channel_id=1, source_target_pairs={{0,3},{1,0},{2,1},{3,2},{4,7},{5,4},{6,5},{7,6},{8,11},{9,8},{10,9... | collective-permute-start | bytes 1179656 | tf_op jit(solution)/shard_map/ppermute | solution.py:565
  38.6 13.9 %collective-permute-start.6 = (bf16[16,1024]{1,0:T(8,128)(2,1)S(1)}, bf16[16,1024]{1,0:T(8,128)(2,1)S(1)}, u32[]{:S(2)}, u32[]{:S(2)}) collective-permute-start(bf16[16,1024]{1,0:T(8,128)(2,1)S(1)} %get-tuple-element.79), channel_id=1, source_target_pairs={{0,4},{4,8},{8,12},{12,16},{16,20},{20,24},{24,28},{28,32},{32,36}... | collective-permute-start | bytes 98312 | tf_op jit(solution)/shard_map/ppermute | solution.py:597
  61.0 0.8 copy-start
  61.8 22.8 %all-to-all-start = ((bf16[64,16,128]{2,1,0:T(8,128)(2,1)}), bf16[64,16,128]{2,1,0:T(8,128)(2,1)}, u32[]{:S(2)}, u32[]{:S(2)}) async-start(bf16[64,16,128]{2,1,0:T(8,128)(2,1)} %get-tuple-element.81), calls=%async_computation | async-start | bytes 524288 | tf_op jit(solution)/shard_map/all_to_all | solution.py:603
  74.8 18.2 %copy-start.17 = (f32[768]{0:T(1024)S(1)}, f32[768]{0:T(1024)}, u32[]{:S(2)}) copy-start(f32[768]{0:T(1024)} %param.22) | copy-start | bytes 9220
  86.8 18.1 %all-to-all-start.1 = ((bf16[64,16,128]{2,1,0:T(8,128)(2,1)}), bf16[64,16,128]{2,1,0:T(8,128)(2,1)}, u32[]{:S(2)}, u32[]{:S(2)}) async-start(bf16[64,16,128]{2,1,0:T(8,128)(2,1)} %scan.1), calls=%async_computation.1 | async-start | bytes 524288 | tf_op jit(solution)/shard_map/all_to_all | solution.py:613
  104.9 1.0 copy-start.1
  112.0 12.1 %collective-permute-start.8 = (bf16[528,384]{1,0:T(8,128)(2,1)}, bf16[528,384]{1,0:T(8,128)(2,1)}, u32[]{:S(2)}, u32[]{:S(2)}) collective-permute-start(bf16[528,384]{1,0:T(8,128)(2,1)} %get-tuple-element.100), channel_id=1, source_target_pairs={{0,1},{1,2},{2,3},{3,0},{4,5},{5,6},{6,7},{7,4},{8,9},{9,10},{10,1... | collective-permute-start | bytes 1216520 | tf_op jit(solution)/shard_map/ppermute | solution.py:562
  118.3 10.9 %collective-permute-start.11 = (bf16[528,384]{1,0:T(8,128)(2,1)}, bf16[528,384]{1,0:T(8,128)(2,1)S(1)}, u32[]{:S(2)}, u32[]{:S(2)}) collective-permute-start(bf16[528,384]{1,0:T(8,128)(2,1)} %get-tuple-element.108), channel_id=1, source_target_pairs={{0,3},{1,0},{2,1},{3,2},{4,7},{5,4},{6,5},{7,6},{8,11},{9,8},{10,9... | collective-permute-start | bytes 1216520 | tf_op jit(solution)/shard_map/ppermute | solution.py:565
  120.9 17.0 %collective-permute-start.7 = (bf16[528,384]{1,0:T(8,128)(2,1)}, bf16[528,384]{1,0:T(8,128)(2,1)S(1)}, u32[]{:S(2)}, u32[]{:S(2)}) collective-permute-start(bf16[528,384]{1,0:T(8,128)(2,1)} %get-tuple-element.98), channel_id=1, source_target_pairs={{0,3},{1,0},{2,1},{3,2},{4,7},{5,4},{6,5},{7,6},{8,11},{9,8},{10,9... | collective-permute-start | bytes 1216520 | tf_op jit(solution)/shard_map/ppermute | solution.py:565
  121.2 16.8 %collective-permute-start.10 = (bf16[528,384]{1,0:T(8,128)(2,1)}, bf16[528,384]{1,0:T(8,128)(2,1)S(1)}, u32[]{:S(2)}, u32[]{:S(2)}) collective-permute-start(bf16[528,384]{1,0:T(8,128)(2,1)} %get-tuple-element.106), channel_id=1, source_target_pairs={{0,1},{1,2},{2,3},{3,0},{4,5},{5,6},{6,7},{7,4},{8,9},{9,10},{10,1... | collective-permute-start | bytes 1216520 | tf_op jit(solution)/shard_map/ppermute | solution.py:562
  126.0 14.8 %collective-permute-start.9 = (bf16[528,384]{1,0:T(8,128)(2,1)}, bf16[528,384]{1,0:T(8,128)(2,1)S(1)}, u32[]{:S(2)}, u32[]{:S(2)}) collective-permute-start(bf16[528,384]{1,0:T(8,128)(2,1)} %add.37), channel_id=1, source_target_pairs={{0,1},{1,2},{2,3},{3,0},{4,5},{5,6},{6,7},{7,4},{8,9},{9,10},{10,1... | collective-permute-start | bytes 1216520 | tf_op jit(solution)/shard_map/ppermute | solution.py:562
  129.2 0.8 copy-start.15
  132.0 14.6 %collective-permute-start.12 = (bf16[528,384]{1,0:T(8,128)(2,1)}, bf16[528,384]{1,0:T(8,128)(2,1)S(1)}, u32[]{:S(2)}, u32[]{:S(2)}) collective-permute-start(bf16[528,384]{1,0:T(8,128)(2,1)} %add.38), channel_id=1, source_target_pairs={{0,3},{1,0},{2,1},{3,2},{4,7},{5,4},{6,5},{7,6},{8,11},{9,8},{10,9... | collective-permute-start | bytes 1216520 | tf_op jit(solution)/shard_map/ppermute | solution.py:565
  137.9 8.7 %copy-start.11 = (bf16[528,384]{1,0:T(8,128)(2,1)}, bf16[528,384]{1,0:T(8,128)(2,1)S(1)}, u32[]{:S(2)}) copy-start(bf16[528,384]{1,0:T(8,128)(2,1)S(1)} %collective-permute-done.7.direct_a) | copy-start | bytes 1216516
  137.9 8.7 %copy-start.12 = (bf16[528,384]{1,0:T(8,128)(2,1)}, bf16[528,384]{1,0:T(8,128)(2,1)S(1)}, u32[]{:S(2)}) copy-start(bf16[528,384]{1,0:T(8,128)(2,1)S(1)} %collective-permute-done.10.direct_b) | copy-start | bytes 1216516
  140.8 5.8 %copy-start.13 = (bf16[528,384]{1,0:T(8,128)(2,1)}, bf16[528,384]{1,0:T(8,128)(2,1)S(1)}, u32[]{:S(2)}) copy-start(bf16[528,384]{1,0:T(8,128)(2,1)S(1)} %collective-permute-done.9.arrived_a) | copy-start | bytes 1216516
  146.6 0.8 copy-start.14
where the time goes:
time: 152 us; the launch traced here: 150 us
  Pallas kernels  62.5 us (41%)
  starting transfers between devices  40.5 us (27%)
  waiting for transfers between devices  32 us (21%)
  local copies, waits for them, and re-layouts  14.7 us (10%)
    pallas_call x2, Pallas kernels, front(): pl.pallas_call(functools.partial(front_kernel, inner, last), grid_spec=pl...  17 us
    pallas_call x2, Pallas kernels, gather(): pl.pallas_call(gather_kernel, grid_spec=pltpu.PrefetchScalarGridSpec(num_...  15.4 us
    ppermute x6, starting transfers between devices, left(): return lax.ppermute(v, 'head', to_left)  13.6 us
    pallas_call x2, Pallas kernels, tail(): pl.pallas_call(functools.partial(tail_kernel, inner, half), grid=(grid,),...  12.3 us
    ppermute x6, waiting for transfers between devices, left(): return lax.ppermute(v, 'head', to_left)  11.7 us
    all_to_all x1, starting transfers between devices, per_device(): taken = lax.all_to_all(payload, 'ctx', 0, 0)  10.9 us
    unnamed x37, local copies, waits for them, and re-layouts  10.3 us
    all_to_all x1, waiting for transfers between devices, per_device(): incoming = lax.all_to_all(scan(taken, thrice), 'ctx', 0, 0)  8.01 us
  transfers between devices with their start and end apart: 15, of which 8 were waited for; matrix products, arithmetic and copies ran while one was open for 5% of the time, Pallas kernels for 28%

commit v1 on v0

--- a/solution.py
+++ b/solution.py
@@ -126,7 +126,9 @@
     ]
     return pl.pallas_call(
         functools.partial(prepare_kernel, heads, inner, blocks),
-        out_shape=[jax.ShapeDtypeStruct(*v) for v in shapes],
+        out_shape=[
+            (jax.ShapeDtypeStruct if k == 3 else far_memory)(*v) for k, v in enumerate(shapes)
+        ],
         compiler_params=pltpu.CompilerParams(vmem_limit_bytes=VMEM),
         cost_estimate=LIGHT,
         name="prepare",
@@ -138,28 +140,19 @@
     acc, acc_others, squares, lhs,
 ):
     width = own.shape[1]
-    step = pl.program_id(0)
-
-    @pl.when(step == 0)
-    def _():
-        square = None
-        for k, (piece, gain) in enumerate(((own, gain_0), (from_left, gain_1), (from_right, gain_2))):
-            values = piece[...].astype(f32)
-            lhs[:, k * width : (k + 1) * width] = (values * gain[0]).astype(bf16)
-            part = jnp.sum(values * values, axis=1, keepdims=True)
-            square = part if square is None else square + part
-        squares[...] = square
-
-    acc[0] = jnp.dot(
+    square = None
+    for k, (piece, gain) in enumerate(((own, gain_0), (from_left, gain_1), (from_right, gain_2))):
+        values = piece[...].astype(f32)
+        lhs[:, k * width : (k + 1) * width] = (values * gain[0]).astype(bf16)
+        part = jnp.sum(values * values, axis=1, keepdims=True)
+        square = part if square is None else square + part
+    squares[...] = square
+    acc[...] = jnp.dot(
         lhs[...], jnp.concatenate([w_0[0], w_1[0], w_2[0]], axis=0), preferred_element_type=f32
     )
-
-    @pl.when(step == 1)
-    def _():
-        acc_others[...] = jnp.dot(
-            lhs[...], jnp.concatenate([o_0[...], o_1[...], o_2[...]], axis=0),
-            preferred_element_type=f32,
-        )
+    acc_others[...] = jnp.dot(
+        lhs[...], jnp.concatenate([o_0[...], o_1[...], o_2[...]], axis=0), preferred_element_type=f32
+    )
 
 
 def gather(owners, own, from_left, from_right, gains, gate_x, others):
@@ -174,7 +167,7 @@
         return pl.BlockSpec((1, 1, width), lambda n, o: (o[k], 0, 0))
 
     def wide(k):
-        return pl.BlockSpec((1, width, inner), lambda n, o: (n, o[k], 0))
+        return pl.BlockSpec((1, width, inner), lambda n, o: (1, o[k], 0))
 
     def small(k):
         return pl.BlockSpec((width, narrow), lambda n, o: (o[k], 0))
@@ -183,20 +176,67 @@
         gather_kernel,
         grid_spec=pltpu.PrefetchScalarGridSpec(
             num_scalar_prefetch=1,
-            grid=(2,),
+            grid=(1,),
             in_specs=[whole(rows, width)] * 3 + [f(k) for f in (gain, wide, small) for k in range(3)],
             out_specs=[
-                pl.BlockSpec((1, rows, inner), lambda n, o: (n, 0, 0)), whole(rows, narrow), whole(rows, 1),
+                whole(rows, inner), whole(rows, narrow), whole(rows, 1),
             ],
             scratch_shapes=[pltpu.VMEM((rows, 3 * width), bf16)],
         ),
         out_shape=[
-            far_memory((2, rows, inner), f32), far_memory((rows, narrow), f32), far_memory((rows, 1), f32),
+            far_memory((rows, inner), f32), far_memory((rows, narrow), f32), far_memory((rows, 1), f32),
         ],
         compiler_params=pltpu.CompilerParams(vmem_limit_bytes=VMEM),
         cost_estimate=LIGHT,
         name="gather",
     )(owners, own, from_left, from_right, gains, gains, gains, gate_x, gate_x, gate_x, others, others, others)
+
+
+def gate_kernel(
+    owners, own, from_left, from_right, far, gain_0, gain_1, gain_2, gain_3, w_0, w_1, w_2, w_3,
+    squares, out, lhs,
+):
+    width = own.shape[1]
+    for k, (piece, gain) in enumerate(
+        ((own, gain_0), (from_left, gain_1), (from_right, gain_2), (far, gain_3))
+    ):
+        values = piece[...].astype(f32)
+        lhs[:, k * width : (k + 1) * width] = (values * gain[0]).astype(bf16)
+    square = squares[...] + jnp.sum(values * values, axis=1, keepdims=True)
+    full = jnp.dot(
+        lhs[...], jnp.concatenate([w_0[0], w_1[0], w_2[0], w_3[0]], axis=0), preferred_element_type=f32
+    )
+    out[...] = (full * lax.rsqrt(square * (1.0 / D) + eps)).astype(bf16)
+
+
+def project_gate(rows, owners, pieces, gains, gate_x, squares):
+    width = pieces[0].shape[1]
+    inner = gate_x.shape[2]
+    grid = rows // BLOCK
+
+    def row(width):
+        return pl.BlockSpec((BLOCK, width), lambda i, o: (i, 0))
+
+    def gain(k):
+        return pl.BlockSpec((1, 1, width), lambda i, o: (o[k], 0, 0))
+
+    def wide(k):
+        return pl.BlockSpec((1, width, inner), lambda i, o: (0, o[k], 0))
+
+    return pl.pallas_call(
+        gate_kernel,
+        grid_spec=pltpu.PrefetchScalarGridSpec(
+            num_scalar_prefetch=1,
+            grid=(grid,),
+            in_specs=[row(width)] * 4 + [f(k) for f in (gain, wide) for k in range(4)] + [row(1)],
+            out_specs=row(inner),
+            scratch_shapes=[pltpu.VMEM((BLOCK, 4 * width), bf16)],
+        ),
+        out_shape=far_memory((rows, inner), bf16),
+        compiler_params=pltpu.CompilerParams(vmem_limit_bytes=VMEM),
+        cost_estimate=LIGHT,
+        name="gate",
+    )(owners, *pieces, *[gains] * 4, *[gate_x] * 4, squares)
 
 
 def front_kernel(
@@ -205,9 +245,9 @@
     *rest,
 ):
     if last:
-        later, join, gate, x_out, bc_out, xs_out, entering, state, payload, extended, slabs = rest
+        later, join, x_out, bc_out, xs_out, entering, state, payload, extended, slabs = rest
     else:
-        rim_acc, rim_others, rim_piece, rim_squares, gate, x_out, bc_out, xs_out, entering, state, tail, extended = rest
+        rim_acc, rim_others, rim_piece, rim_squares, x_out, bc_out, xs_out, entering, state, tail, extended = rest
     index = pl.program_id(0)
     wide = inner + 2 * STATE
 
@@ -230,7 +270,7 @@
         else:
             values, lhs = scaled(rim_piece)
             scale = row_scale(rim_squares, values)
-            x_rim = (rim_acc[1] + dot(lhs, gate_x[1])) * scale
+            x_rim = (rim_acc[...] + dot(lhs, gate_x[0])) * scale
             bc_rim = (
                 rim_others[:, : 2 * STATE] + dot(lhs, others[:, : 2 * STATE])
             ) * scale
@@ -243,8 +283,7 @@
 
     values, lhs = scaled(piece)
     scale = row_scale(squares, values)
-    gate[...] = ((acc[0] + dot(lhs, gate_x[0])) * scale).astype(bf16)
-    x_raw = ((acc[1] + dot(lhs, gate_x[1])) * scale).astype(bf16)
+    x_raw = ((acc[...] + dot(lhs, gate_x[0])) * scale).astype(bf16)
     others_raw = ((acc_others[...] + dot(lhs, others[...])) * scale).astype(bf16)
     extended[RIM : RIM + BLOCK, :inner] = x_raw.astype(f32)
     extended[RIM : RIM + BLOCK, inner:] = others_raw[:, : 2 * STATE].astype(f32)
@@ -313,8 +352,7 @@
     else:
         operands = (acc, acc_others, piece, squares)
         extra = [
-            pl.BlockSpec((2, RIM, inner), lambda i, o: (0, rows // RIM, 0)),
-            rim(acc_others.shape[1]), rim(width), rim(1),
+            rim(inner), rim(acc_others.shape[1]), rim(width), rim(1),
         ]
         out_spec, out_shape = whole(RIM, wide), (RIM, wide)
         scratch = []
@@ -324,24 +362,23 @@
             num_scalar_prefetch=1,
             grid=(grid,),
             in_specs=[
-                pl.BlockSpec((2, BLOCK, inner), lambda i, o: (0, i, 0)), row(acc_others.shape[1]),
+                row(inner), row(acc_others.shape[1]),
                 row(width), row(1),
                 pl.BlockSpec((1, 1, width), lambda i, o: (o[0], 0, 0)),
-                pl.BlockSpec((2, width, inner), lambda i, o: (0, o[0], 0)),
+                pl.BlockSpec((1, width, inner), lambda i, o: (1, o[0], 0)),
                 pl.BlockSpec((width, others.shape[1]), lambda i, o: (o[0], 0)),
                 whole(RIM, wide), whole(CONV + 1, wide),
                 whole(1, LANES), row(LANES, base), whole(2 * LANES, inner),
                 pl.BlockSpec((1, 1, inner), lambda i, o: (i + base, 0, 0)), whole(1, LANES),
             ] + extra,
             out_specs=[
-                row(inner), row(inner), row(2 * STATE), row(inner),
+                row(inner), row(2 * STATE), row(inner),
                 pl.BlockSpec((1, STATE, inner), lambda i, o: (i, 0, 0)),
                 whole(STATE, inner), out_spec,
             ],
             scratch_shapes=[pltpu.VMEM((BLOCK + RIM, wide), f32)] + scratch,
         ),
         out_shape=[
-            far_memory((rows, inner), bf16),
             far_memory((rows, inner), bf16),
             far_memory((rows, 2 * STATE), bf16),
             far_memory((rows, inner), bf16),
@@ -381,6 +418,8 @@
         functools.partial(scan_kernel, chunks),
         out_shape=jax.ShapeDtypeStruct(taken.shape, bf16),
         scratch_shapes=[pltpu.VMEM(taken.shape, f32), pltpu.VMEM(taken.shape, f32)],
+        compiler_params=pltpu.CompilerParams(vmem_limit_bytes=VMEM // 2),
+        cost_estimate=LIGHT,
         name="scan",
     )(taken, spread)
 
@@ -429,7 +468,7 @@
 def tail_kernel(
     inner, half_index,
     y_in, x_conv, gate, bc, entering, taken, earlier, fade_in, before, skip, decay, spread, gain, weight,
-    far, right, left, own, squares, slabs, incoming,
+    far, scaled_out, squares, slabs, incoming,
 ):
     chunks = inner // LANES
 
@@ -455,19 +494,16 @@
     scaled = (gated * gain[...]).astype(bf16)
     width = far.shape[1]
     place = pl.ds(pl.multiple_of(step * BLOCK, BLOCK), BLOCK)
-    outs = (own, right, far, left)
-    for n, out in enumerate(outs):
-        out[place] = jnp.dot(
-            scaled, weight[:, n * width : (n + 1) * width], preferred_element_type=f32
-        ).astype(bf16)
+    far[place] = jnp.dot(scaled, weight[...], preferred_element_type=f32).astype(bf16)
+    scaled_out[place] = scaled
 
     @pl.when(step == pl.num_programs(0) - 1)
     def _():
         rows = far.shape[0] - 16
         parts = coded(squares[...])
-        for out in outs:
+        for out in (far, scaled_out):
             out[rows : rows + 16, :BLOCK] = parts
-            out[rows : rows + 16, BLOCK:] = jnp.zeros((16, width - BLOCK), bf16)
+            out[rows : rows + 16, BLOCK:] = jnp.zeros((16, out.shape[1] - BLOCK), bf16)
 
 
 def tail(half, y_in, x_conv, gate, bc, entering, taken, earlier, channels, decay, spread, gain, weight):
@@ -495,15 +531,18 @@
             pl.BlockSpec((1, STATE, inner), lambda i: (i, 0, 0)),
             whole(*taken.shape), whole(STATE, inner), channel(2 * blocks), channel(blocks + base, 1),
             channel(2 * blocks + 2), row(LANES, base), whole(2 * LANES, inner), whole(1, inner),
-            whole(*weight.shape),
+            pl.BlockSpec((inner, width), lambda i: (0, 2)),
         ],
-        out_specs=[whole(rows + 16, width)] * 4,
-        out_shape=[far_memory((rows + 16, width), bf16)] * 4,
+        out_specs=[whole(rows + 16, width), whole(rows + 16, inner)],
+        out_shape=[far_memory((rows + 16, width), bf16), far_memory((rows + 16, inner), bf16)],
         scratch_shapes=[
             pltpu.VMEM((8, BLOCK), f32), pltpu.VMEM(taken.shape, f32), pltpu.VMEM((STATE, inner), f32),
         ],
         compiler_params=pltpu.CompilerParams(vmem_limit_bytes=VMEM),
-        cost_estimate=LIGHT,
+        cost_estimate=pl.CostEstimate(
+            flops=2 * rows * inner * (weight.shape[1] + STATE),
+            bytes_accessed=rows * inner * 10 + weight.size * 2, transcendentals=rows * inner,
+        ),
         name="tail",
     )(
         y_in, x_conv, gate, bc, entering, taken, earlier, channels, channels, channels, decay, spread, gain,
@@ -511,6 +550,31 @@
     )
 
 
+def rest_kernel(scaled_b, scaled_a, weight, right_b, left_b, own_b, left_a, right_a, own_a):
+    width = own_a.shape[1]
+    for scaled, outs in ((scaled_b, (own_b, right_b, left_b)), (scaled_a, (own_a, right_a, left_a))):
+        rows = scaled.shape[0] - 16
+        for n, out in zip((0, 1, 3), outs):
+            out[:rows] = jnp.dot(
+                scaled[:rows], weight[:, n * width : (n + 1) * width], preferred_element_type=f32
+            ).astype(bf16)
+            out[rows:] = scaled[rows:, :width]
+
+
+def rest(scaled_b, scaled_a, weight):
+    shape = jax.ShapeDtypeStruct((scaled_a.shape[0], weight.shape[1] // 4), bf16)
+    return pl.pallas_call(
+        rest_kernel,
+        out_shape=[shape] * 6,
+        compiler_params=pltpu.CompilerParams(vmem_limit_bytes=VMEM),
+        cost_estimate=pl.CostEstimate(
+            flops=3 * scaled_a.size * weight.shape[1], bytes_accessed=4 * scaled_a.size + 2 * weight.size,
+            transcendentals=0,
+        ),
+        name="rest",
+    )(scaled_b, scaled_a, weight)
+
+
 def add_kernel(u, v, out):
     rows = out.shape[0] - 16
     out[:rows] = (u[:rows].astype(f32) + v[:rows].astype(f32)).astype(bf16)
@@ -519,7 +583,8 @@
 
 def add(u, v):
     return pl.pallas_call(
-        add_kernel, out_shape=jax.ShapeDtypeStruct(u.shape, bf16), cost_estimate=LIGHT, name="add"
+        add_kernel, out_shape=jax.ShapeDtypeStruct(u.shape, bf16), cost_estimate=LIGHT, name="add",
+        compiler_params=pltpu.CompilerParams(vmem_limit_bytes=VMEM // 2),
     )(u, v)
 
 
@@ -539,6 +604,7 @@
     rows, width = parts[0].shape
     return pl.pallas_call(
         finish_kernel, out_shape=jax.ShapeDtypeStruct((2 * (rows - 16), width), bf16),
+        compiler_params=pltpu.CompilerParams(vmem_limit_bytes=VMEM // 2),
         cost_estimate=LIGHT, name="finish",
     )(*parts)
 
@@ -570,13 +636,17 @@
     gains = norm_gain.reshape(groups, 1, width)
     owners = jnp.stack([me, lax.rem(me + groups - 1, groups), lax.rem(me + 1, groups)]).astype(jnp.int32)
     owner = lax.rem(me + 2, groups).astype(jnp.int32)[None]
-    right_bottom, hidden, gate_x, log_decay, dt_weight, bc_weight = lax.optimization_barrier(
-        (right_bottom, hidden, gate_x, log_decay, dt_weight, bc_weight)
-    )
-    decay, decay_t, to_end, channels, total, spread, thrice, others, taps, bias = prepare(
-        jnp.transpose(log_decay), jnp.transpose(dt_weight), bc_weight, conv_x, conv_bc,
-        dt_bias[None], skip_gain[None],
-    )
+    all_owners = jnp.concatenate([owners, owner])
+    prepared = prepare(
+        *kept(
+            jnp.transpose(log_decay), jnp.transpose(dt_weight), bc_weight, conv_x, conv_bc,
+            dt_bias[None], skip_gain[None],
+        )
+    )
+    right_bottom, hidden, gate_x, prepared = lax.optimization_barrier(
+        (right_bottom, hidden, gate_x, prepared)
+    )
+    decay, decay_t, to_end, channels, total, spread, thrice, others, taps, bias = prepared
     gate_x, = kept(gate_x)
     far_bottom = right(right_bottom)
     top = hidden[:middle]
@@ -590,13 +660,13 @@
     gain = out_gain[None]
 
     no_rim = jnp.zeros((RIM, inner + 2 * STATE), bf16)
-    gate_b, x_b, bc_b, xs_b, enter_b, state_b, raw_tail = front(
+    x_b, bc_b, xs_b, enter_b, state_b, raw_tail = front(
         False, 1, owner, *kept(acc_b, others_b), far_bottom, *kept(squares_b), gains, gate_x, others, no_rim, taps,
         bias, to_end, spread, channels, total,
     )
     near = lax.ppermute(raw_tail, "ctx", [(i, i + 1) for i in range(places - 1)])
     acc_a, others_a, squares_a = gather(owners, top, right_top, left_top, gains, gate_x, others)
-    gate_a, x_a, bc_a, xs_a, enter_a, state_a, payload = front(
+    x_a, bc_a, xs_a, enter_a, state_a, payload = front(
         True, 0, owner, *kept(acc_a, others_a), far_top, *kept(squares_a), gains, gate_x, others, near, taps, bias,
         to_end, spread, channels, total, state_b, channels,
     )
@@ -609,21 +679,30 @@
         ],
         axis=1,
     )
-    taken, inside_a, turned = lax.optimization_barrier((taken, inside_a, turned))
+    gate_a = project_gate(
+        middle, all_owners, kept(top, right_top, left_top, far_top), gains, gate_x, *kept(squares_a)
+    )
+    taken, inside_a, turned, gate_a = lax.optimization_barrier((taken, inside_a, turned, gate_a))
     incoming = lax.all_to_all(scan(taken, thrice), "ctx", 0, 0)
     inside_b = inside(*kept(bc_b, xs_b), decay, decay_t, 1)
-    incoming, inside_b = lax.optimization_barrier((incoming, inside_b))
-
-    far_a, right_a, left_a, own_a = tail(
+    gate_b = project_gate(
+        middle, all_owners, kept(bottom, right_bottom, left_bottom, far_bottom), gains, gate_x,
+        *kept(squares_b),
+    )
+    incoming, inside_b, gate_b = lax.optimization_barrier((incoming, inside_b, gate_b))
+
+    far_b, scaled_b = tail(
+        1, *kept(inside_b, x_b, gate_b, bc_b, enter_b), incoming, *kept(state_a), channels, decay,
+        spread, gain, turned,
+    )
+    far_a, scaled_a = tail(
         0, *kept(inside_a, x_a, gate_a, bc_a, enter_a), incoming, state_a, channels, decay, spread,
         gain, turned,
     )
-    passed_a, direct_a = right(far_a), left(left_a)
-    far_b, right_b, left_b, own_b = tail(
-        1, *kept(inside_b, x_b, gate_b, bc_b, enter_b), incoming, *kept(state_a), channels, decay,
-        spread, gain, turned,
-    )
-    passed_b, direct_b = left(far_b), right(right_b)
+    passed_b = left(far_b)
+    passed_a = right(far_a)
+    right_b, left_b, own_b, left_a, right_a, own_a = rest(scaled_b, scaled_a, turned)
+    direct_a, direct_b = left(left_a), right(right_b)
     arrived_a = right(add(right_a, passed_a))
     arrived_b = left(add(left_b, passed_b))
     return finish(own_a, direct_a, arrived_a, own_b, direct_b, arrived_b)

time: 152 us -> 146 us (0.961)
  waiting for transfers between devices: 32 us -> 25.2 us
  starting transfers between devices: 40.5 us -> 42.6 us
    pallas_call x0 -> x3, Pallas kernels: none -> 12.8 us  [the longest x2 10.2 us: project_gate(): pl.pallas_call(gate_kernel, grid_spec=pltpu.PrefetchScalarGridSpec(num_sc...]
    ppermute x6, waiting for transfers between devices: 6.49 us -> 17.9 us  [right(): return lax.ppermute(v, 'head', to_right)]
    ppermute x6, waiting for transfers between devices: 11.7 us -> 4.43 us  [left(): return lax.ppermute(v, 'head', to_left)]
    all_to_all x1, waiting for transfers between devices: 5.89 us -> 0.01 us  [per_device(): taken = lax.all_to_all(payload, 'ctx', 0, 0)]
    pallas_call x2, Pallas kernels: 15.4 us -> 10.3 us  [gather(): pl.pallas_call(gather_kernel, grid_spec=pltpu.PrefetchScalarGridSpec(num_...]
    all_to_all x1, waiting for transfers between devices: 8.01 us -> 2.91 us  [per_device(): incoming = lax.all_to_all(scan(taken, thrice), 'ctx', 0, 0)]
    all_to_all x1, starting transfers between devices: 6.22 us -> 10.5 us  [per_device(): incoming = lax.all_to_all(scan(taken, thrice), 'ctx', 0, 0)]
    pallas_call x2, Pallas kernels: 3.95 us -> 0.22 us  [add(): pl.pallas_call(add_kernel, out_shape=jax.ShapeDtypeStruct(u.shape, bf16),...]
  transfers between devices with their start and end apart: 15 -> 15, of which waited for: 8 -> 6; matrix products, arithmetic and copies ran while one was open for 5% -> 5% of each run, Pallas kernels for 28% -> 32%
where the time goes in v1:
time: 146 us; the launch traced here: 145 us
  Pallas kernels  61.8 us (42%)
  starting transfers between devices  42.6 us (29%)
  waiting for transfers between devices  25.2 us (17%)
  local copies, waits for them, and re-layouts  14.4 us (10%)
    ppermute x6, waiting for transfers between devices, right(): return lax.ppermute(v, 'head', to_right)  17.9 us
    pallas_call x2, Pallas kernels, front(): pl.pallas_call(functools.partial(front_kernel, inner, last), grid_spec=pl...  15 us
    ppermute x6, starting transfers between devices, left(): return lax.ppermute(v, 'head', to_left)  11 us
    all_to_all x1, starting transfers between devices, per_device(): taken = lax.all_to_all(payload, 'ctx', 0, 0)  10.9 us
    unnamed x45, local copies, waits for them, and re-layouts  10.7 us
    all_to_all x1, starting transfers between devices, per_device(): incoming = lax.all_to_all(scan(taken, thrice), 'ctx', 0, 0)  10.5 us
    pallas_call x2, Pallas kernels, gather(): pl.pallas_call(gather_kernel, grid_spec=pltpu.PrefetchScalarGridSpec(num_...  10.3 us
    pallas_call x2, Pallas kernels, project_gate(): pl.pallas_call(gate_kernel, grid_spec=pltpu.PrefetchScalarGridSpec(num_sc...  10.2 us
  transfers between devices with their start and end apart: 15, of which 6 were waited for; matrix products, arithmetic and copies ran while one was open for 5% of the time, Pallas kernels for 32%

profile of v1, /device:TPU:1, one launch (start us, length us, event | category | flops | bytes accessed | tf_op | source)
XLA Modules:
  0.0 144.9 jit_solution(4550501480210955054)
XLA Ops:
  0.0 1.0 slice.9
  1.0 0.7 slice.10
  1.8 0.0 copy-start.4
  1.8 2.2 %collective-permute-start = (bf16[528,384]{1,0:T(8,128)(2,1)S(1)}, bf16[528,384]{1,0:T(8,128)(2,1)S(1)}, u32[]{:S(2)}, u32[]{:S(2)}) collective-permute-start(bf16[528,384]{1,0:T(8,128)(2,1)S(1)} %pad_maximum_fusion.1.own), channel_id=1, source_target_pairs={{0,1},{1,2},{2,3},{3,0},{4,5},{5,6},{6,7},{7,4},{8,9},{9,10},{10,1... | collective-permute-start | bytes 1216520 | tf_op jit(solution)/shard_map/ppermute | solution.py:628
  4.0 1.5 %collective-permute-start.2 = (bf16[528,384]{1,0:T(8,128)(2,1)S(1)}, bf16[528,384]{1,0:T(8,128)(2,1)}, u32[]{:S(2)}, u32[]{:S(2)}) collective-permute-start(bf16[528,384]{1,0:T(8,128)(2,1)S(1)} %pad_maximum_fusion.1.own), channel_id=1, source_target_pairs={{0,3},{1,0},{2,1},{3,2},{4,7},{5,4},{6,5},{7,6},{8,11},{9,8},{10,9... | collective-permute-start | bytes 1216520 | tf_op jit(solution)/shard_map/ppermute | solution.py:631
  5.5 3.5 %prepare.1 = (f32[1024,128]{1,0:T(8,128)}, f32[16,1024]{1,0:T(8,128)}, f32[1024,128]{1,0:T(8,128)}, f32[16,768]{1,0:T(8,128)S(1)}, f32[1,128]{1,0:T(1,128)}, /*i...) custom-call(f32[12,1024]{1,0:T(8,128)} %bitcast.27, ...), custom_call_target="tpu_custom_call" | custom-call | flops 1024 | bytes 1024 | tf_op jit(solution)/shard_map/prepare/pallas_call | solution.py:127
  9.0 5.2 %copy.15 = bf16[1536,2,768]{2,0,1:T(8,128)(2,1)} copy(bf16[1536,2,768]{2,1,0:T(2,128)(2,1)} %param.14) | data formatting | bytes 9437184 | tf_op args[2]
  14.3 0.0 collective-permute-done.from_left
  14.3 0.0 copy-start.5
  14.3 1.6 %collective-permute-start.1 = (bf16[512,384]{1,0:T(8,128)(2,1)S(1)}, bf16[512,384]{1,0:T(8,128)(2,1)}, u32[]{:S(2)}, u32[]{:S(2)}) collective-permute-start(bf16[512,384]{1,0:T(8,128)(2,1)S(1)} %slice.11.own), channel_id=1, source_target_pairs={{0,3},{1,0},{2,1},{3,2},{4,7},{5,4},{6,5},{7,6},{8,11},{9,8},{10,9... | collective-permute-start | bytes 1179656 | tf_op jit(solution)/shard_map/ppermute | solution.py:631
  15.9 0.0 collective-permute-start.5
  15.9 0.1 pad_add_fusion.owners
  16.1 0.0 collective-permute-done.2.from_right
  16.1 5.1 %gather.2 = (f32[528,768]{1,0:T(8,128)}, f32[528,384]{1,0:T(8,128)}, f32[528,1]{1,0:T(8,128)}) custom-call(s32[3]{0:T(128)S(1)} %pad_add_fusion.owners, bf16[528,384]{1,0:T(8,128)(2,1)S(1)} %pad_maximum_fusion.1.own, bf16[528,384]{1,0:T(8,128)(2,1)S(1)} %collective-permute-done.from_left, bf16[528,384]{1,0:T(8,128)(2,1)} %collective-permute-done.2.from_right, ...), custom_call_target="tpu_custom_call" | custom-call | flops 1024 | bytes 1024 | tf_op jit(solution)/shard_map/gather/pallas_call | solution.py:175
  21.2 0.0 copy-done.7
  21.2 1.7 %collective-permute-done.1.from_right = bf16[512,384]{1,0:T(8,128)(2,1)} collective-permute-done((bf16[512,384]{1,0:T(8,128)(2,1)S(1)}, bf16[512,384]{1,0:T(8,128)(2,1)}, u32[]{:S(2)}, u32[]{:S(2)}) %collective-permute-start.1) | collective-permute-done | bytes 393248 | tf_op jit(solution)/shard_map/ppermute | solution.py:631
  22.9 0.6 collective-permute-start.3
  23.5 3.0 %collective-permute-start.4 = (bf16[512,384]{1,0:T(8,128)(2,1)}, bf16[512,384]{1,0:T(8,128)(2,1)S(1)}, u32[]{:S(2)}, u32[]{:S(2)}) collective-permute-start(bf16[512,384]{1,0:T(8,128)(2,1)} %collective-permute-done.1.from_right), channel_id=1, source_target_pairs={{0,3},{1,0},{2,1},{3,2},{4,7},{5,4},{6,5},{7,6},{8,11},{9,8},{10,9... | collective-permute-start | bytes 1179656 | tf_op jit(solution)/shard_map/ppermute | solution.py:631
  26.5 0.0 collective-permute-done.5.piece.rest_2_.far
  26.5 0.0 copy-start.6
  26.5 1.1 copy-done.6
  27.7 7.3 %front.2 = (bf16[512,768]{1,0:T(8,128)(2,1)}, bf16[512,256]{1,0:T(8,128)(2,1)}, bf16[512,768]{1,0:T(8,128)(2,1)}, f32[2,128,768]{2,1,0:T(8,128)}, f32[128,768]{1,0:T(8,128)S(1)}, /*index=5*/bf16[16,1024]{1,0:T(8,128)(2,1)S(1)}) custom-call(s32[1]{0:T(128)} %bitcast.owner, f32[528,768]{1,0:T(8,128)} %get-tuple-element.86.acc.rest_0_, ...), custom_call_target="tpu_custom_call" | custom-call | flops 1024 | bytes 1024 | tf_op jit(solution)/shard_map/front/pallas_call | solution.py:359
  34.9 0.0 copy-done.3
  34.9 6.9 %collective-permute-start.6 = (bf16[16,1024]{1,0:T(8,128)(2,1)S(1)}, bf16[16,1024]{1,0:T(8,128)(2,1)S(1)}, u32[]{:S(2)}, u32[]{:S(2)}) collective-permute-start(bf16[16,1024]{1,0:T(8,128)(2,1)S(1)} %get-tuple-element.95), channel_id=1, source_target_pairs={{0,4},{4,8},{8,12},{12,16},{16,20},{20,24},{24,28},{28,32},{32,36}... | collective-permute-start | bytes 98312 | tf_op jit(solution)/shard_map/ppermute | solution.py:667
  41.8 0.0 collective-permute-done.3.from_left
  41.9 5.2 %gather.3 = (f32[512,768]{1,0:T(8,128)}, f32[512,384]{1,0:T(8,128)}, f32[512,1]{1,0:T(8,128)}) custom-call(s32[3]{0:T(128)S(1)} %pad_add_fusion.owners, bf16[512,384]{1,0:T(8,128)(2,1)S(1)} %slice.11.own, bf16[512,384]{1,0:T(8,128)(2,1)} %collective-permute-done.3.from_left, bf16[512,384]{1,0:T(8,128)(2,1)} %collective-permute-done.1.from_right, ...), custom_call_target="tpu_custom_call" | custom-call | flops 1024 | bytes 1024 | tf_op jit(solution)/shard_map/gather/pallas_call | solution.py:175
  47.0 0.0 collective-permute-done.6.near
  47.0 0.0 collective-permute-done.4.piece.far
  47.1 7.8 %front.3 = (bf16[512,768]{1,0:T(8,128)(2,1)}, bf16[512,256]{1,0:T(8,128)(2,1)}, bf16[512,768]{1,0:T(8,128)(2,1)}, f32[2,128,768]{2,1,0:T(8,128)}, f32[128,768]{1,0:T(8,128)S(1)}, /*index=5*/bf16[64,16,128]{2,1,0:T(8,128)(2,1)}) custom-call(s32[1]{0:T(128)} %bitcast.owner, f32[512,768]{1,0:T(8,128)} %get-tuple-element.83.acc, ...), custom_call_target="tpu_custom_call" | custom-call | flops 1024 | bytes 1024 | tf_op jit(solution)/shard_map/front/pallas_call | solution.py:359
  54.9 0.7 copy-done.8
  55.6 10.9 %all-to-all-start = ((bf16[64,16,128]{2,1,0:T(8,128)(2,1)}), bf16[64,16,128]{2,1,0:T(8,128)(2,1)}, u32[]{:S(2)}, u32[]{:S(2)}) async-start(bf16[64,16,128]{2,1,0:T(8,128)(2,1)} %get-tuple-element.97), calls=%async_computation | async-start | bytes 524288 | tf_op jit(solution)/shard_map/all_to_all | solution.py:673
  66.5 0.1 pad_add_fusion.1.owners
  66.6 1.9 %constant_dynamic-slice_fusion.3 = (bf16[768,384]{1,0:T(8,128)(2,1)S(1)}, bf16[768,384]{1,0:T(8,128)(2,1)S(1)}, bf16[768,384]{1,0:T(8,128)(2,1)S(1)}, bf16[768,384]{1,0:T(8,128)(2,1)S(1)}) fusion(bf16[768,1536]{1,0:T(8,128)(2,1)} %param.23, s32[]{:T(128)S(6)} %select_n.12, s32[]{:T(128)S(6)} %select_n.13, s32[]{:T(128)S(6)} %select_n.15, s32[]{:T(128)S(6)} %select_n.14), kind=kLoop, calls=%fused_computation.6 | loop fusion | bytes 4718608 | tf_op jit(solution)/shard_map/dynamic_slice | solution.py:677
  68.5 0.2 pad_maximum_fusion.weight
  68.7 0.8 copy-done.1
  69.5 3.9 %inside.2.y_in = f32[512,768]{1,0:T(8,128)} custom-call(bf16[512,256]{1,0:T(8,128)(2,1)} %get-tuple-element.98.bc, bf16[512,768]{1,0:T(8,128)(2,1)} %get-tuple-element.99.xs, f32[1024,128]{1,0:T(8,128)S(1)} %copy-done.1, f32[16,1024]{1,0:T(8,128)S(1)} %copy-done.12), custom_call_target="tpu_custom_call" | custom-call | flops 1024 | bytes 1024 | tf_op jit(solution)/shard_map/inside/pallas_call | solution.py:451
  73.4 5.2 %gate.2 = bf16[512,768]{1,0:T(8,128)(2,1)} custom-call(s32[4]{0:T(128)S(1)} %pad_add_fusion.1.owners, bf16[512,384]{1,0:T(8,128)(2,1)} %copy-done.5, bf16[512,384]{1,0:T(8,128)(2,1)} %collective-permute-done.3.from_left, bf16[512,384]{1,0:T(8,128)(2,1)} %collective-permute-done.1.from_right, bf16[512,384]{1,0:T(8,128)(2,1)} %copy-done.10, ...), custom_call_target="tpu_custom_call" | custom-call | flops 1024 | bytes 1024 | tf_op jit(solution)/shard_map/gate/pallas_call | solution.py:226
  78.5 0.0 all-to-all-done.taken
  78.5 0.9 copy-done.13
  79.5 1.4 scan.1
  80.9 0.7 copy-done.11
  81.6 10.5 %all-to-all-start.1 = ((bf16[64,16,128]{2,1,0:T(8,128)(2,1)}), bf16[64,16,128]{2,1,0:T(8,128)(2,1)}, u32[]{:S(2)}, u32[]{:S(2)}) async-start(bf16[64,16,128]{2,1,0:T(8,128)(2,1)} %copy-done.11), calls=%async_computation.1 | async-start | bytes 524288 | tf_op jit(solution)/shard_map/all_to_all | solution.py:686
  92.1 4.0 %inside.3.y_in = f32[512,768]{1,0:T(8,128)} custom-call(bf16[512,256]{1,0:T(8,128)(2,1)} %get-tuple-element.104.bc, bf16[512,768]{1,0:T(8,128)(2,1)} %get-tuple-element.105.xs, f32[1024,128]{1,0:T(8,128)S(1)} %copy-done.1, f32[16,1024]{1,0:T(8,128)S(1)} %copy-done.12), custom_call_target="tpu_custom_call" | custom-call | flops 1024 | bytes 1024 | tf_op jit(solution)/shard_map/inside/pallas_call | solution.py:451
  96.1 5.0 %gate.3 = bf16[512,768]{1,0:T(8,128)(2,1)} custom-call(s32[4]{0:T(128)S(1)} %pad_add_fusion.1.owners, bf16[528,384]{1,0:T(8,128)(2,1)} %copy-done.4, bf16[528,384]{1,0:T(8,128)(2,1)} %copy-done.7, bf16[528,384]{1,0:T(8,128)(2,1)} %collective-permute-done.2.from_right, bf16[528,384]{1,0:T(8,128)(2,1)} %copy-done.3, ...), custom_call_target="tpu_custom_call" | custom-call | flops 1024 | bytes 1024 | tf_op jit(solution)/shard_map/gate/pallas_call | solution.py:226
  101.1 2.9 %all-to-all-done.1.taken = bf16[64,16,128]{2,1,0:T(8,128)(2,1)} async-done(((bf16[64,16,128]{2,1,0:T(8,128)(2,1)}), bf16[64,16,128]{2,1,0:T(8,128)(2,1)}, u32[]{:S(2)}, u32[]{:S(2)}) %all-to-all-start.1) | async-done | bytes 262176 | tf_op jit(solution)/shard_map/all_to_all | solution.py:686
  104.0 4.8 %tail.2 = (bf16[528,384]{1,0:T(8,128)(2,1)}, bf16[528,768]{1,0:T(8,128)(2,1)}) custom-call(f32[512,768]{1,0:T(8,128)} %inside.3.y_in, bf16[512,768]{1,0:T(8,128)(2,1)} %get-tuple-element.107.x_conv, bf16[512,768]{1,0:T(8,128)(2,1)} %gate.3, bf16[512,256]{1,0:T(8,128)(2,1)} %get-tuple-element.104.bc, f32[2,128,768]{2,1,0:T(8,128)} %get-tuple-element.109.entering, ...), custom_call_target="tpu_custom_call" | custom-call | flops 1308622848 | bytes 6291456 | tf_op jit(solution)/shard_map/tail/pallas_call | solution.py:526
  108.8 1.1 collective-permute-start.11
  109.9 4.6 %tail.3 = (bf16[528,384]{1,0:T(8,128)(2,1)}, bf16[528,768]{1,0:T(8,128)(2,1)}) custom-call(f32[512,768]{1,0:T(8,128)} %inside.2.y_in, bf16[512,768]{1,0:T(8,128)(2,1)} %get-tuple-element.115.x_conv, bf16[512,768]{1,0:T(8,128)(2,1)} %gate.2, bf16[512,256]{1,0:T(8,128)(2,1)} %get-tuple-element.98.bc, f32[2,128,768]{2,1,0:T(8,128)} %get-tuple-element.117.entering, ...), custom_call_target="tpu_custom_call" | custom-call | flops 1308622848 | bytes 6291456 | tf_op jit(solution)/shard_map/tail/pallas_call | solution.py:526
  114.5 0.4 collective-permute-start.8
  114.9 1.1 copy-done.18
  116.0 2.6 %rest.1 = (bf16[528,384]{1,0:T(8,128)(2,1)S(1)}, bf16[528,384]{1,0:T(8,128)(2,1)S(1)}, bf16[528,384]{1,0:T(8,128)(2,1)S(1)}, bf16[528,384]{1,0:T(8,128)(2,1)S(1)...) custom-call(bf16[528,768]{1,0:T(8,128)(2,1)S(1)} %copy-done.17, bf16[528,768]{1,0:T(8,128)(2,1)S(1)} %copy-done.18, ...), custom_call_target="tpu_custom_call" | custom-call | flops 1868562432 | bytes 3981312 | tf_op jit(solution)/shard_map/rest/pallas_call | solution.py:566
  118.6 0.1 collective-permute-start.10
  118.7 2.7 %collective-permute-start.7 = (bf16[528,384]{1,0:T(8,128)(2,1)S(1)}, bf16[528,384]{1,0:T(8,128)(2,1)S(1)}, u32[]{:S(2)}, u32[]{:S(2)}) collective-permute-start(bf16[528,384]{1,0:T(8,128)(2,1)S(1)} %get-tuple-element.120), channel_id=1, source_target_pairs={{0,3},{1,0},{2,1},{3,2},{4,7},{5,4},{6,5},{7,6},{8,11},{9,8},{10,9... | collective-permute-start | bytes 1216520 | tf_op jit(solution)/shard_map/ppermute | solution.py:631
  121.4 0.0 collective-permute-done.11.v
  121.4 0.1 add.44
  121.5 1.2 collective-permute-start.12
  122.7 3.4 %collective-permute-done.8.v = bf16[528,384]{1,0:T(8,128)(2,1)S(1)} collective-permute-done((bf16[528,384]{1,0:T(8,128)(2,1)}, bf16[528,384]{1,0:T(8,128)(2,1)S(1)}, u32[]{:S(2)}, u32[]{:S(2)}) %collective-permute-start.8) | collective-permute-done | bytes 405536 | tf_op jit(solution)/shard_map/ppermute | solution.py:628
  126.1 0.1 add.43
  126.2 0.1 collective-permute-start.9
  126.3 8.5 %collective-permute-done.10.direct_b = bf16[528,384]{1,0:T(8,128)(2,1)S(1)} collective-permute-done((bf16[528,384]{1,0:T(8,128)(2,1)S(1)}, bf16[528,384]{1,0:T(8,128)(2,1)S(1)}, u32[]{:S(2)}, u32[]{:S(2)}) %collective-permute-start.10) | collective-permute-done | bytes 405536 | tf_op jit(solution)/shard_map/ppermute | solution.py:628
  134.8 0.0 collective-permute-done.7.direct_a
  134.8 2.7 %collective-permute-done.12.arrived_b = bf16[528,384]{1,0:T(8,128)(2,1)S(1)} collective-permute-done((bf16[528,384]{1,0:T(8,128)(2,1)S(1)}, bf16[528,384]{1,0:T(8,128)(2,1)S(1)}, u32[]{:S(2)}, u32[]{:S(2)}) %collective-permute-start.12) | collective-permute-done | bytes 405536 | tf_op jit(solution)/shard_map/ppermute | solution.py:631
  137.5 6.0 %collective-permute-done.9.arrived_a = bf16[528,384]{1,0:T(8,128)(2,1)S(1)} collective-permute-done((bf16[528,384]{1,0:T(8,128)(2,1)S(1)}, bf16[528,384]{1,0:T(8,128)(2,1)S(1)}, u32[]{:S(2)}, u32[]{:S(2)}) %collective-permute-start.9) | collective-permute-done | bytes 405536 | tf_op jit(solution)/shard_map/ppermute | solution.py:628
  143.5 1.4 finish.1
  (39 shorter events, 0.2 us)
Async XLA Ops:
  1.8 14.3 %copy-start.4 = (bf16[528,384]{1,0:T(8,128)(2,1)}, bf16[528,384]{1,0:T(8,128)(2,1)S(1)}, u32[]{:S(2)}) copy-start(bf16[528,384]{1,0:T(8,128)(2,1)S(1)} %pad_maximum_fusion.1.own) | copy-start | bytes 1216516
  1.8 12.5 %collective-permute-start = (bf16[528,384]{1,0:T(8,128)(2,1)S(1)}, bf16[528,384]{1,0:T(8,128)(2,1)S(1)}, u32[]{:S(2)}, u32[]{:S(2)}) collective-permute-start(bf16[528,384]{1,0:T(8,128)(2,1)S(1)} %pad_maximum_fusion.1.own), channel_id=1, source_target_pairs={{0,1},{1,2},{2,3},{3,0},{4,5},{5,6},{6,7},{7,4},{8,9},{9,10},{10,1... | collective-permute-start | bytes 1216520 | tf_op jit(solution)/shard_map/ppermute | solution.py:628
  4.0 12.1 %collective-permute-start.2 = (bf16[528,384]{1,0:T(8,128)(2,1)S(1)}, bf16[528,384]{1,0:T(8,128)(2,1)}, u32[]{:S(2)}, u32[]{:S(2)}) collective-permute-start(bf16[528,384]{1,0:T(8,128)(2,1)S(1)} %pad_maximum_fusion.1.own), channel_id=1, source_target_pairs={{0,3},{1,0},{2,1},{3,2},{4,7},{5,4},{6,5},{7,6},{8,11},{9,8},{10,9... | collective-permute-start | bytes 1216520 | tf_op jit(solution)/shard_map/ppermute | solution.py:631
  9.0 5.3 %copy-start.19 = (bf16[1024,384]{1,0:T(8,128)(2,1)S(1)}, bf16[1024,384]{1,0:T(8,128)(2,1)}, u32[]{:S(2)}) copy-start(bf16[1024,384]{1,0:T(8,128)(2,1)} %param.12) | copy-start | bytes 2359300
  9.0 7.0 %copy-start.20 = (f32[1536]{0:T(1024)S(1)}, f32[1536]{0:T(1024)}, u32[]{:S(2)}) copy-start(f32[1536]{0:T(1024)} %param.13) | copy-start | bytes 18436
  9.0 7.1 %copy-start = (bf16[1536,384]{1,0:T(8,128)(2,1)S(1)}, bf16[1536,384]{1,0:T(8,128)(2,1)}, u32[]{:S(2)}) copy-start(bf16[1536,384]{1,0:T(8,128)(2,1)} %get-tuple-element.79.o_0.o_1.o_2.others) | copy-start | bytes 3538948
  14.3 6.9 %copy-start.7 = (bf16[528,384]{1,0:T(8,128)(2,1)}, bf16[528,384]{1,0:T(8,128)(2,1)S(1)}, u32[]{:S(2)}) copy-start(bf16[528,384]{1,0:T(8,128)(2,1)S(1)} %collective-permute-done.from_left) | copy-start | bytes 1216516
  14.3 27.5 %copy-start.5 = (bf16[512,384]{1,0:T(8,128)(2,1)}, bf16[512,384]{1,0:T(8,128)(2,1)S(1)}, u32[]{:S(2)}) copy-start(bf16[512,384]{1,0:T(8,128)(2,1)S(1)} %slice.11.own) | copy-start | bytes 1179652
  14.3 8.6 %collective-permute-start.1 = (bf16[512,384]{1,0:T(8,128)(2,1)S(1)}, bf16[512,384]{1,0:T(8,128)(2,1)}, u32[]{:S(2)}, u32[]{:S(2)}) collective-permute-start(bf16[512,384]{1,0:T(8,128)(2,1)S(1)} %slice.11.own), channel_id=1, source_target_pairs={{0,3},{1,0},{2,1},{3,2},{4,7},{5,4},{6,5},{7,6},{8,11},{9,8},{10,9... | collective-permute-start | bytes 1179656 | tf_op jit(solution)/shard_map/ppermute | solution.py:631
  15.9 10.5 %collective-permute-start.5 = (bf16[528,384]{1,0:T(8,128)(2,1)S(1)}, bf16[528,384]{1,0:T(8,128)(2,1)S(1)}, u32[]{:S(2)}, u32[]{:S(2)}) collective-permute-start(bf16[528,384]{1,0:T(8,128)(2,1)S(1)} %collective-permute-done.from_left), channel_id=1, source_target_pairs={{0,1},{1,2},{2,3},{3,0},{4,5},{5,6},{6,7},{7,4},{8,9},{9,10},{10,1... | collective-permute-start | bytes 1216520 | tf_op jit(solution)/shard_map/ppermute | solution.py:628
  16.0 10.5 %copy-start.2 = (bf16[256,768]{1,0:T(8,128)(2,1)S(1)}, bf16[256,768]{1,0:T(8,128)(2,1)}, u32[]{:S(2)}) copy-start(bf16[256,768]{1,0:T(8,128)(2,1)} %get-tuple-element.92.spread) | copy-start | bytes 1179652
  16.0 10.5 %copy-start.14 = (f32[5,1024]{1,0:T(8,128)S(1)}, f32[5,1024]{1,0:T(8,128)}, u32[]{:S(2)}) copy-start(f32[5,1024]{1,0:T(8,128)} %get-tuple-element.89.taps) | copy-start | bytes 61444
  16.1 10.5 %copy-start.15 = (f32[1,128]{1,0:T(1,128)S(1)}, f32[1,128]{1,0:T(1,128)}, u32[]{:S(2)}) copy-start(f32[1,128]{1,0:T(1,128)} %get-tuple-element.94.total) | copy-start | bytes 1540
  16.1 10.5 %copy-start.16 = (f32[1,128]{1,0:T(1,128)S(1)}, f32[1,128]{1,0:T(1,128)}, u32[]{:S(2)}) copy-start(f32[1,128]{1,0:T(1,128)} %get-tuple-element.90.dt_bias) | copy-start | bytes 1540
  22.9 18.9 %collective-permute-start.3 = (bf16[512,384]{1,0:T(8,128)(2,1)S(1)}, bf16[512,384]{1,0:T(8,128)(2,1)}, u32[]{:S(2)}, u32[]{:S(2)}) collective-permute-start(bf16[512,384]{1,0:T(8,128)(2,1)S(1)} %slice.11.own), channel_id=1, source_target_pairs={{0,1},{1,2},{2,3},{3,0},{4,5},{5,6},{6,7},{7,4},{8,9},{9,10},{10,1... | collective-permute-start | bytes 1179656 | tf_op jit(solution)/shard_map/ppermute | solution.py:628
  23.5 23.6 %collective-permute-start.4 = (bf16[512,384]{1,0:T(8,128)(2,1)}, bf16[512,384]{1,0:T(8,128)(2,1)S(1)}, u32[]{:S(2)}, u32[]{:S(2)}) collective-permute-start(bf16[512,384]{1,0:T(8,128)(2,1)} %collective-permute-done.1.from_right), channel_id=1, source_target_pairs={{0,3},{1,0},{2,1},{3,2},{4,7},{5,4},{6,5},{7,6},{8,11},{9,8},{10,9... | collective-permute-start | bytes 1179656 | tf_op jit(solution)/shard_map/ppermute | solution.py:631
  26.5 8.5 %copy-start.3 = (bf16[528,384]{1,0:T(8,128)(2,1)}, bf16[528,384]{1,0:T(8,128)(2,1)S(1)}, u32[]{:S(2)}) copy-start(bf16[528,384]{1,0:T(8,128)(2,1)S(1)} %collective-permute-done.5.piece.rest_2_.far) | copy-start | bytes 1216516
  26.5 1.1 copy-start.6
  34.9 12.1 %collective-permute-start.6 = (bf16[16,1024]{1,0:T(8,128)(2,1)S(1)}, bf16[16,1024]{1,0:T(8,128)(2,1)S(1)}, u32[]{:S(2)}, u32[]{:S(2)}) collective-permute-start(bf16[16,1024]{1,0:T(8,128)(2,1)S(1)} %get-tuple-element.95), channel_id=1, source_target_pairs={{0,4},{4,8},{8,12},{12,16},{16,20},{20,24},{24,28},{28,32},{32,36}... | collective-permute-start | bytes 98312 | tf_op jit(solution)/shard_map/ppermute | solution.py:667
  47.1 7.8 %copy-start.10 = (bf16[512,384]{1,0:T(8,128)(2,1)}, bf16[512,384]{1,0:T(8,128)(2,1)S(1)}, u32[]{:S(2)}) copy-start(bf16[512,384]{1,0:T(8,128)(2,1)S(1)} %collective-permute-done.4.piece.far) | copy-start | bytes 1179652
  54.9 0.7 copy-start.8
  55.6 22.9 %all-to-all-start = ((bf16[64,16,128]{2,1,0:T(8,128)(2,1)}), bf16[64,16,128]{2,1,0:T(8,128)(2,1)}, u32[]{:S(2)}, u32[]{:S(2)}) async-start(bf16[64,16,128]{2,1,0:T(8,128)(2,1)} %get-tuple-element.97), calls=%async_computation | async-start | bytes 524288 | tf_op jit(solution)/shard_map/all_to_all | solution.py:673
  68.4 1.0 copy-start.1
  68.4 1.0 copy-start.12
  73.4 18.7 %copy-start.21 = (f32[768]{0:T(1024)S(1)}, f32[768]{0:T(1024)}, u32[]{:S(2)}) copy-start(f32[768]{0:T(1024)} %param.22) | copy-start | bytes 9220
  78.5 0.9 copy-start.13
  80.9 0.7 copy-start.11
  81.6 22.4 %all-to-all-start.1 = ((bf16[64,16,128]{2,1,0:T(8,128)(2,1)}), bf16[64,16,128]{2,1,0:T(8,128)(2,1)}, u32[]{:S(2)}, u32[]{:S(2)}) async-start(bf16[64,16,128]{2,1,0:T(8,128)(2,1)} %copy-done.11), calls=%async_computation.1 | async-start | bytes 524288 | tf_op jit(solution)/shard_map/all_to_all | solution.py:686
  104.0 5.9 %copy-start.9 = (f32[128,768]{1,0:T(8,128)S(1)}, f32[128,768]{1,0:T(8,128)}, u32[]{:S(2)}) copy-start(f32[128,768]{1,0:T(8,128)} %copy-done.8) | copy-start | bytes 1179652
  108.8 12.6 %collective-permute-start.11 = (bf16[528,384]{1,0:T(8,128)(2,1)}, bf16[528,384]{1,0:T(8,128)(2,1)S(1)}, u32[]{:S(2)}, u32[]{:S(2)}) collective-permute-start(bf16[528,384]{1,0:T(8,128)(2,1)} %get-tuple-element.126), channel_id=1, source_target_pairs={{0,3},{1,0},{2,1},{3,2},{4,7},{5,4},{6,5},{7,6},{8,11},{9,8},{10,9... | collective-permute-start | bytes 1216520 | tf_op jit(solution)/shard_map/ppermute | solution.py:631
  109.9 5.0 %copy-start.17 = (bf16[528,768]{1,0:T(8,128)(2,1)S(1)}, bf16[528,768]{1,0:T(8,128)(2,1)}, u32[]{:S(2)}) copy-start(bf16[528,768]{1,0:T(8,128)(2,1)} %get-tuple-element.113.scaled_b) | copy-start | bytes 2433028
  114.5 11.6 %collective-permute-start.8 = (bf16[528,384]{1,0:T(8,128)(2,1)}, bf16[528,384]{1,0:T(8,128)(2,1)S(1)}, u32[]{:S(2)}, u32[]{:S(2)}) collective-permute-start(bf16[528,384]{1,0:T(8,128)(2,1)} %get-tuple-element.122), channel_id=1, source_target_pairs={{0,1},{1,2},{2,3},{3,0},{4,5},{5,6},{6,7},{7,4},{8,9},{9,10},{10,1... | collective-permute-start | bytes 1216520 | tf_op jit(solution)/shard_map/ppermute | solution.py:628
  114.9 1.1 copy-start.18
  118.6 16.1 %collective-permute-start.10 = (bf16[528,384]{1,0:T(8,128)(2,1)S(1)}, bf16[528,384]{1,0:T(8,128)(2,1)S(1)}, u32[]{:S(2)}, u32[]{:S(2)}) collective-permute-start(bf16[528,384]{1,0:T(8,128)(2,1)S(1)} %get-tuple-element.124), channel_id=1, source_target_pairs={{0,1},{1,2},{2,3},{3,0},{4,5},{5,6},{6,7},{7,4},{8,9},{9,10},{10,1... | collective-permute-start | bytes 1216520 | tf_op jit(solution)/shard_map/ppermute | solution.py:628
  118.7 16.0 %collective-permute-start.7 = (bf16[528,384]{1,0:T(8,128)(2,1)S(1)}, bf16[528,384]{1,0:T(8,128)(2,1)S(1)}, u32[]{:S(2)}, u32[]{:S(2)}) collective-permute-start(bf16[528,384]{1,0:T(8,128)(2,1)S(1)} %get-tuple-element.120), channel_id=1, source_target_pairs={{0,3},{1,0},{2,1},{3,2},{4,7},{5,4},{6,5},{7,6},{8,11},{9,8},{10,9... | collective-permute-start | bytes 1216520 | tf_op jit(solution)/shard_map/ppermute | solution.py:631
  121.5 16.0 %collective-permute-start.12 = (bf16[528,384]{1,0:T(8,128)(2,1)S(1)}, bf16[528,384]{1,0:T(8,128)(2,1)S(1)}, u32[]{:S(2)}, u32[]{:S(2)}) collective-permute-start(bf16[528,384]{1,0:T(8,128)(2,1)S(1)} %add.44), channel_id=1, source_target_pairs={{0,3},{1,0},{2,1},{3,2},{4,7},{5,4},{6,5},{7,6},{8,11},{9,8},{10,9... | collective-permute-start | bytes 1216520 | tf_op jit(solution)/shard_map/ppermute | solution.py:631
  126.2 17.3 %collective-permute-start.9 = (bf16[528,384]{1,0:T(8,128)(2,1)S(1)}, bf16[528,384]{1,0:T(8,128)(2,1)S(1)}, u32[]{:S(2)}, u32[]{:S(2)}) collective-permute-start(bf16[528,384]{1,0:T(8,128)(2,1)S(1)} %add.43), channel_id=1, source_target_pairs={{0,1},{1,2},{2,3},{3,0},{4,5},{5,6},{6,7},{7,4},{8,9},{9,10},{10,1... | collective-permute-start | bytes 1216520 | tf_op jit(solution)/shard_map/ppermute | solution.py:628

commit v2 on v1

--- a/solution.py
+++ b/solution.py
@@ -383,7 +383,7 @@
             far_memory((rows, 2 * STATE), bf16),
             far_memory((rows, inner), bf16),
             far_memory((grid, STATE, inner), f32),
-            jax.ShapeDtypeStruct((STATE, inner), f32),
+            far_memory((STATE, inner), f32),
             jax.ShapeDtypeStruct(out_shape, bf16),
         ],
         compiler_params=pltpu.CompilerParams(vmem_limit_bytes=VMEM),
@@ -662,16 +662,16 @@
     no_rim = jnp.zeros((RIM, inner + 2 * STATE), bf16)
     x_b, bc_b, xs_b, enter_b, state_b, raw_tail = front(
         False, 1, owner, *kept(acc_b, others_b), far_bottom, *kept(squares_b), gains, gate_x, others, no_rim, taps,
-        bias, to_end, spread, channels, total,
+        bias, *kept(to_end), spread, channels, total,
     )
     near = lax.ppermute(raw_tail, "ctx", [(i, i + 1) for i in range(places - 1)])
     acc_a, others_a, squares_a = gather(owners, top, right_top, left_top, gains, gate_x, others)
     x_a, bc_a, xs_a, enter_a, state_a, payload = front(
         True, 0, owner, *kept(acc_a, others_a), far_top, *kept(squares_a), gains, gate_x, others, near, taps, bias,
-        to_end, spread, channels, total, state_b, channels,
+        *kept(to_end), spread, channels, total, state_b, channels,
     )
     taken = lax.all_to_all(payload, "ctx", 0, 0)
-    inside_a = inside(*kept(bc_a, xs_a), decay, decay_t, 0)
+    inside_a = inside(*kept(bc_a, xs_a, decay, decay_t), 0)
     turned = jnp.concatenate(
         [
             lax.dynamic_slice_in_dim(out_weight, lax.rem(me + k, groups) * width, width, 1)
@@ -683,8 +683,8 @@
         middle, all_owners, kept(top, right_top, left_top, far_top), gains, gate_x, *kept(squares_a)
     )
     taken, inside_a, turned, gate_a = lax.optimization_barrier((taken, inside_a, turned, gate_a))
-    incoming = lax.all_to_all(scan(taken, thrice), "ctx", 0, 0)
-    inside_b = inside(*kept(bc_b, xs_b), decay, decay_t, 1)
+    incoming = lax.all_to_all(scan(taken, *kept(thrice)), "ctx", 0, 0)
+    inside_b = inside(*kept(bc_b, xs_b, decay, decay_t), 1)
     gate_b = project_gate(
         middle, all_owners, kept(bottom, right_bottom, left_bottom, far_bottom), gains, gate_x,
         *kept(squares_b),

time: 146 us -> 142 us (0.973)
  local copies, waits for them, and re-layouts: 14.4 us -> 10.1 us
    unnamed x45 -> x35, local copies, waits for them, and re-layouts: 10.7 us -> 6.42 us
  transfers between devices with their start and end apart: 15 -> 15, of which waited for: 6 -> 7; matrix products, arithmetic and copies ran while one was open for 5% -> 5% of each run, Pallas kernels for 32% -> 33%
where the time goes in v2:
time: 142 us; the launch traced here: 141 us
  Pallas kernels  62.9 us (44%)
  starting transfers between devices  41.8 us (29%)
  waiting for transfers between devices  25.9 us (18%)
  local copies, waits for them, and re-layouts  10.1 us (7%)
    ppermute x6, waiting for transfers between devices, right(): return lax.ppermute(v, 'head', to_right)  17.6 us
    pallas_call x2, Pallas kernels, front(): pl.pallas_call(functools.partial(front_kernel, inner, last), grid_spec=pl...  15.4 us
    all_to_all x1, starting transfers between devices, per_device(): taken = lax.all_to_all(payload, 'ctx', 0, 0)  10.7 us
    pallas_call x2, Pallas kernels, gather(): pl.pallas_call(gather_kernel, grid_spec=pltpu.PrefetchScalarGridSpec(num_...  10.3 us
    ppermute x6, starting transfers between devices, left(): return lax.ppermute(v, 'head', to_left)  10.3 us
    pallas_call x2, Pallas kernels, project_gate(): pl.pallas_call(gate_kernel, grid_spec=pltpu.PrefetchScalarGridSpec(num_sc...  10.1 us
    all_to_all x1, starting transfers between devices, per_device(): incoming = lax.all_to_all(scan(taken, *kept(thrice)), 'ctx', 0, 0)  9.69 us
    pallas_call x2, Pallas kernels, tail(): pl.pallas_call(functools.partial(tail_kernel, inner, half), grid=(grid,),...  9.33 us
  transfers between devices with their start and end apart: 15, of which 7 were waited for; matrix products, arithmetic and copies ran while one was open for 5% of the time, Pallas kernels for 33%

profile of v2, /device:TPU:1, one launch (start us, length us, event | category | flops | bytes accessed | tf_op | source)
XLA Modules:
  0.0 141.4 jit_solution(9991140748446494497)
XLA Ops:
  0.0 1.0 slice.9
  1.0 0.7 slice.10
  1.8 0.0 copy-start.4
  1.8 2.2 %collective-permute-start = (bf16[528,384]{1,0:T(8,128)(2,1)S(1)}, bf16[528,384]{1,0:T(8,128)(2,1)}, u32[]{:S(2)}, u32[]{:S(2)}) collective-permute-start(bf16[528,384]{1,0:T(8,128)(2,1)S(1)} %pad_maximum_fusion.1.own), channel_id=1, source_target_pairs={{0,1},{1,2},{2,3},{3,0},{4,5},{5,6},{6,7},{7,4},{8,9},{9,10},{10,1... | collective-permute-start | bytes 1216520 | tf_op jit(solution)/shard_map/ppermute | solution.py:628
  4.0 1.5 %collective-permute-start.2 = (bf16[528,384]{1,0:T(8,128)(2,1)S(1)}, bf16[528,384]{1,0:T(8,128)(2,1)}, u32[]{:S(2)}, u32[]{:S(2)}) collective-permute-start(bf16[528,384]{1,0:T(8,128)(2,1)S(1)} %pad_maximum_fusion.1.own), channel_id=1, source_target_pairs={{0,3},{1,0},{2,1},{3,2},{4,7},{5,4},{6,5},{7,6},{8,11},{9,8},{10,9... | collective-permute-start | bytes 1216520 | tf_op jit(solution)/shard_map/ppermute | solution.py:631
  5.5 3.5 %prepare.1 = (f32[1024,128]{1,0:T(8,128)}, f32[16,1024]{1,0:T(8,128)}, f32[1024,128]{1,0:T(8,128)}, f32[16,768]{1,0:T(8,128)S(1)}, f32[1,128]{1,0:T(1,128)}, /*i...) custom-call(f32[12,1024]{1,0:T(8,128)} %bitcast.27, ...), custom_call_target="tpu_custom_call" | custom-call | flops 1024 | bytes 1024 | tf_op jit(solution)/shard_map/prepare/pallas_call | solution.py:127
  9.0 0.0 copy-start
  9.1 5.2 %copy.15 = bf16[1536,2,768]{2,0,1:T(8,128)(2,1)} copy(bf16[1536,2,768]{2,1,0:T(2,128)(2,1)} %param.14) | data formatting | bytes 9437184 | tf_op args[2]
  14.3 0.0 collective-permute-done.from_left
  14.3 0.0 copy-done.14
  14.3 0.0 copy-start.5
  14.3 1.6 %collective-permute-start.1 = (bf16[512,384]{1,0:T(8,128)(2,1)S(1)}, bf16[512,384]{1,0:T(8,128)(2,1)}, u32[]{:S(2)}, u32[]{:S(2)}) collective-permute-start(bf16[512,384]{1,0:T(8,128)(2,1)S(1)} %slice.11.own), channel_id=1, source_target_pairs={{0,3},{1,0},{2,1},{3,2},{4,7},{5,4},{6,5},{7,6},{8,11},{9,8},{10,9... | collective-permute-start | bytes 1179656 | tf_op jit(solution)/shard_map/ppermute | solution.py:631
  15.9 0.0 collective-permute-start.5
  15.9 0.1 pad_add_fusion.owners
  16.0 0.0 copy-done.15
  16.0 0.0 copy-start.2
  16.0 0.0 copy-start.9
  16.1 0.0 copy-start.10
  16.1 0.0 copy-start.11
  16.1 0.0 collective-permute-done.2.from_right
  16.1 5.2 %gather.2 = (f32[528,768]{1,0:T(8,128)}, f32[528,384]{1,0:T(8,128)}, f32[528,1]{1,0:T(8,128)}) custom-call(s32[3]{0:T(128)S(1)} %pad_add_fusion.owners, bf16[528,384]{1,0:T(8,128)(2,1)S(1)} %pad_maximum_fusion.1.own, bf16[528,384]{1,0:T(8,128)(2,1)} %collective-permute-done.from_left, bf16[528,384]{1,0:T(8,128)(2,1)} %collective-permute-done.2.from_right, ...), custom_call_target="tpu_custom_call" | custom-call | flops 1024 | bytes 1024 | tf_op jit(solution)/shard_map/gather/pallas_call | solution.py:175
  21.3 1.5 %collective-permute-done.1.from_right = bf16[512,384]{1,0:T(8,128)(2,1)} collective-permute-done((bf16[512,384]{1,0:T(8,128)(2,1)S(1)}, bf16[512,384]{1,0:T(8,128)(2,1)}, u32[]{:S(2)}, u32[]{:S(2)}) %collective-permute-start.1) | collective-permute-done | bytes 393248 | tf_op jit(solution)/shard_map/ppermute | solution.py:631
  22.8 0.6 collective-permute-start.3
  23.4 2.9 %collective-permute-start.4 = (bf16[512,384]{1,0:T(8,128)(2,1)}, bf16[512,384]{1,0:T(8,128)(2,1)S(1)}, u32[]{:S(2)}, u32[]{:S(2)}) collective-permute-start(bf16[512,384]{1,0:T(8,128)(2,1)} %collective-permute-done.1.from_right), channel_id=1, source_target_pairs={{0,3},{1,0},{2,1},{3,2},{4,7},{5,4},{6,5},{7,6},{8,11},{9,8},{10,9... | collective-permute-start | bytes 1179656 | tf_op jit(solution)/shard_map/ppermute | solution.py:631
  26.4 0.0 collective-permute-done.5.piece.rest_2_.far
  26.4 7.5 %front.2 = (bf16[512,768]{1,0:T(8,128)(2,1)}, bf16[512,256]{1,0:T(8,128)(2,1)}, bf16[512,768]{1,0:T(8,128)(2,1)}, f32[2,128,768]{2,1,0:T(8,128)}, f32[128,768]{1,0:T(8,128)}, /*index=5*/bf16[16,1024]{1,0:T(8,128)(2,1)S(1)}) custom-call(s32[1]{0:T(128)} %bitcast.owner, f32[528,768]{1,0:T(8,128)} %get-tuple-element.86.acc.rest_0_, ...), custom_call_target="tpu_custom_call" | custom-call | flops 1024 | bytes 1024 | tf_op jit(solution)/shard_map/front/pallas_call | solution.py:359
  33.9 7.5 %collective-permute-start.6 = (bf16[16,1024]{1,0:T(8,128)(2,1)S(1)}, bf16[16,1024]{1,0:T(8,128)(2,1)S(1)}, u32[]{:S(2)}, u32[]{:S(2)}) collective-permute-start(bf16[16,1024]{1,0:T(8,128)(2,1)S(1)} %get-tuple-element.95), channel_id=1, source_target_pairs={{0,4},{4,8},{8,12},{12,16},{16,20},{20,24},{24,28},{28,32},{32,36}... | collective-permute-start | bytes 98312 | tf_op jit(solution)/shard_map/ppermute | solution.py:667
  41.4 0.0 collective-permute-done.3.from_left
  41.5 5.1 %gather.3 = (f32[512,768]{1,0:T(8,128)}, f32[512,384]{1,0:T(8,128)}, f32[512,1]{1,0:T(8,128)}) custom-call(s32[3]{0:T(128)S(1)} %pad_add_fusion.owners, bf16[512,384]{1,0:T(8,128)(2,1)S(1)} %slice.11.own, bf16[512,384]{1,0:T(8,128)(2,1)} %collective-permute-done.3.from_left, bf16[512,384]{1,0:T(8,128)(2,1)} %collective-permute-done.1.from_right, ...), custom_call_target="tpu_custom_call" | custom-call | flops 1024 | bytes 1024 | tf_op jit(solution)/shard_map/gather/pallas_call | solution.py:175
  46.6 0.0 collective-permute-done.6.near
  46.6 0.0 collective-permute-done.4.piece.far
  46.6 7.9 %front.3 = (bf16[512,768]{1,0:T(8,128)(2,1)}, bf16[512,256]{1,0:T(8,128)(2,1)}, bf16[512,768]{1,0:T(8,128)(2,1)}, f32[2,128,768]{2,1,0:T(8,128)}, f32[128,768]{1,0:T(8,128)}, /*index=5*/bf16[64,16,128]{2,1,0:T(8,128)(2,1)}) custom-call(s32[1]{0:T(128)} %bitcast.owner, f32[512,768]{1,0:T(8,128)} %get-tuple-element.83.acc, ...), custom_call_target="tpu_custom_call" | custom-call | flops 1024 | bytes 1024 | tf_op jit(solution)/shard_map/front/pallas_call | solution.py:359
  54.5 10.7 %all-to-all-start = ((bf16[64,16,128]{2,1,0:T(8,128)(2,1)}), bf16[64,16,128]{2,1,0:T(8,128)(2,1)S(1)}, u32[]{:S(2)}, u32[]{:S(2)}) async-start(bf16[64,16,128]{2,1,0:T(8,128)(2,1)} %get-tuple-element.97), calls=%async_computation | async-start | bytes 524288 | tf_op jit(solution)/shard_map/all_to_all | solution.py:673
  65.2 0.1 pad_add_fusion.1.owners
  65.3 1.9 %constant_dynamic-slice_fusion.3 = (bf16[768,384]{1,0:T(8,128)(2,1)S(1)}, bf16[768,384]{1,0:T(8,128)(2,1)S(1)}, bf16[768,384]{1,0:T(8,128)(2,1)S(1)}, bf16[768,384]{1,0:T(8,128)(2,1)S(1)}) fusion(bf16[768,1536]{1,0:T(8,128)(2,1)} %param.23, s32[]{:T(128)S(6)} %select_n.12, s32[]{:T(128)S(6)} %select_n.13, s32[]{:T(128)S(6)} %select_n.15, s32[]{:T(128)S(6)} %select_n.14), kind=kLoop, calls=%fused_computation.6 | loop fusion | bytes 4718608 | tf_op jit(solution)/shard_map/dynamic_slice | solution.py:677
  67.2 0.2 pad_maximum_fusion.weight
  67.4 3.9 %inside.2.y_in = f32[512,768]{1,0:T(8,128)} custom-call(bf16[512,256]{1,0:T(8,128)(2,1)} %get-tuple-element.98.bc, bf16[512,768]{1,0:T(8,128)(2,1)} %get-tuple-element.99.xs, f32[1024,128]{1,0:T(8,128)} %get-tuple-element.100.decay, f32[16,1024]{1,0:T(8,128)} %get-tuple-element.101.decay_t), custom_call_target="tpu_custom_call" | custom-call | flops 1024 | bytes 1024 | tf_op jit(solution)/shard_map/inside/pallas_call | solution.py:451
  71.3 5.1 %gate.2 = bf16[512,768]{1,0:T(8,128)(2,1)} custom-call(s32[4]{0:T(128)S(1)} %pad_add_fusion.1.owners, bf16[512,384]{1,0:T(8,128)(2,1)} %copy-done.5, bf16[512,384]{1,0:T(8,128)(2,1)} %collective-permute-done.3.from_left, bf16[512,384]{1,0:T(8,128)(2,1)} %collective-permute-done.1.from_right, bf16[512,384]{1,0:T(8,128)(2,1)} %copy-done.7, ...), custom_call_target="tpu_custom_call" | custom-call | flops 1024 | bytes 1024 | tf_op jit(solution)/shard_map/gate/pallas_call | solution.py:226
  76.4 0.8 all-to-all-done.taken
  77.2 2.1 %scan.1 = bf16[64,16,128]{2,1,0:T(8,128)(2,1)} custom-call(bf16[64,16,128]{2,1,0:T(8,128)(2,1)S(1)} %all-to-all-done.taken, bf16[128,768]{1,0:T(8,128)(2,1)} %get-tuple-element.103.spread), custom_call_target="tpu_custom_call" | custom-call | flops 1024 | bytes 1024 | tf_op jit(solution)/shard_map/scan/pallas_call | solution.py:417
  79.3 9.7 %all-to-all-start.1 = ((bf16[64,16,128]{2,1,0:T(8,128)(2,1)}), bf16[64,16,128]{2,1,0:T(8,128)(2,1)}, u32[]{:S(2)}, u32[]{:S(2)}) async-start(bf16[64,16,128]{2,1,0:T(8,128)(2,1)} %scan.1), calls=%async_computation.1 | async-start | bytes 524288 | tf_op jit(solution)/shard_map/all_to_all | solution.py:686
  89.1 3.9 %inside.3.y_in = f32[512,768]{1,0:T(8,128)} custom-call(bf16[512,256]{1,0:T(8,128)(2,1)} %get-tuple-element.104.bc, bf16[512,768]{1,0:T(8,128)(2,1)} %get-tuple-element.105.xs, f32[1024,128]{1,0:T(8,128)} %get-tuple-element.100.decay, f32[16,1024]{1,0:T(8,128)} %get-tuple-element.101.decay_t), custom_call_target="tpu_custom_call" | custom-call | flops 1024 | bytes 1024 | tf_op jit(solution)/shard_map/inside/pallas_call | solution.py:451
  93.0 5.0 %gate.3 = bf16[512,768]{1,0:T(8,128)(2,1)} custom-call(s32[4]{0:T(128)S(1)} %pad_add_fusion.1.owners, bf16[528,384]{1,0:T(8,128)(2,1)} %copy-done.4, bf16[528,384]{1,0:T(8,128)(2,1)} %collective-permute-done.from_left, bf16[528,384]{1,0:T(8,128)(2,1)} %collective-permute-done.2.from_right, bf16[528,384]{1,0:T(8,128)(2,1)} %copy-done.3, ...), custom_call_target="tpu_custom_call" | custom-call | flops 1024 | bytes 1024 | tf_op jit(solution)/shard_map/gate/pallas_call | solution.py:226
  98.0 2.9 %all-to-all-done.1.taken = bf16[64,16,128]{2,1,0:T(8,128)(2,1)} async-done(((bf16[64,16,128]{2,1,0:T(8,128)(2,1)}), bf16[64,16,128]{2,1,0:T(8,128)(2,1)}, u32[]{:S(2)}, u32[]{:S(2)}) %all-to-all-start.1) | async-done | bytes 262176 | tf_op jit(solution)/shard_map/all_to_all | solution.py:686
  101.0 4.8 %tail.2 = (bf16[528,384]{1,0:T(8,128)(2,1)}, bf16[528,768]{1,0:T(8,128)(2,1)}) custom-call(f32[512,768]{1,0:T(8,128)} %inside.3.y_in, bf16[512,768]{1,0:T(8,128)(2,1)} %get-tuple-element.107.x_conv, bf16[512,768]{1,0:T(8,128)(2,1)} %gate.3, bf16[512,256]{1,0:T(8,128)(2,1)} %get-tuple-element.104.bc, f32[2,128,768]{2,1,0:T(8,128)} %get-tuple-element.109.entering, ...), custom_call_target="tpu_custom_call" | custom-call | flops 1308622848 | bytes 6291456 | tf_op jit(solution)/shard_map/tail/pallas_call | solution.py:526
  105.7 0.7 collective-permute-start.11
  106.5 4.6 %tail.3 = (bf16[528,384]{1,0:T(8,128)(2,1)}, bf16[528,768]{1,0:T(8,128)(2,1)}) custom-call(f32[512,768]{1,0:T(8,128)} %inside.2.y_in, bf16[512,768]{1,0:T(8,128)(2,1)} %get-tuple-element.115.x_conv, bf16[512,768]{1,0:T(8,128)(2,1)} %gate.2, bf16[512,256]{1,0:T(8,128)(2,1)} %get-tuple-element.98.bc, f32[2,128,768]{2,1,0:T(8,128)} %get-tuple-element.117.entering, ...), custom_call_target="tpu_custom_call" | custom-call | flops 1308622848 | bytes 6291456 | tf_op jit(solution)/shard_map/tail/pallas_call | solution.py:526
  111.0 0.8 collective-permute-start.8
  111.8 0.0 copy-done.12
  111.8 1.1 copy-done.13
  112.9 2.6 %rest.1 = (bf16[528,384]{1,0:T(8,128)(2,1)S(1)}, bf16[528,384]{1,0:T(8,128)(2,1)S(1)}, bf16[528,384]{1,0:T(8,128)(2,1)S(1)}, bf16[528,384]{1,0:T(8,128)(2,1)S(1)...) custom-call(bf16[528,768]{1,0:T(8,128)(2,1)S(1)} %copy-done.12, bf16[528,768]{1,0:T(8,128)(2,1)S(1)} %copy-done.13, ...), custom_call_target="tpu_custom_call" | custom-call | flops 1868562432 | bytes 3981312 | tf_op jit(solution)/shard_map/rest/pallas_call | solution.py:566
  115.5 0.1 collective-permute-start.10
  115.6 2.7 %collective-permute-start.7 = (bf16[528,384]{1,0:T(8,128)(2,1)S(1)}, bf16[528,384]{1,0:T(8,128)(2,1)S(1)}, u32[]{:S(2)}, u32[]{:S(2)}) collective-permute-start(bf16[528,384]{1,0:T(8,128)(2,1)S(1)} %get-tuple-element.120), channel_id=1, source_target_pairs={{0,3},{1,0},{2,1},{3,2},{4,7},{5,4},{6,5},{7,6},{8,11},{9,8},{10,9... | collective-permute-start | bytes 1216520 | tf_op jit(solution)/shard_map/ppermute | solution.py:631
  118.3 0.0 collective-permute-done.11.v
  118.3 0.1 add.44
  118.4 0.8 collective-permute-start.12
  119.2 3.4 %collective-permute-done.8.v = bf16[528,384]{1,0:T(8,128)(2,1)S(1)} collective-permute-done((bf16[528,384]{1,0:T(8,128)(2,1)}, bf16[528,384]{1,0:T(8,128)(2,1)S(1)}, u32[]{:S(2)}, u32[]{:S(2)}) %collective-permute-start.8) | collective-permute-done | bytes 405536 | tf_op jit(solution)/shard_map/ppermute | solution.py:628
  122.6 0.1 add.43
  122.7 0.1 collective-permute-start.9
  122.8 8.5 %collective-permute-done.10.direct_b = bf16[528,384]{1,0:T(8,128)(2,1)S(1)} collective-permute-done((bf16[528,384]{1,0:T(8,128)(2,1)S(1)}, bf16[528,384]{1,0:T(8,128)(2,1)S(1)}, u32[]{:S(2)}, u32[]{:S(2)}) %collective-permute-start.10) | collective-permute-done | bytes 405536 | tf_op jit(solution)/shard_map/ppermute | solution.py:628
  131.3 0.0 collective-permute-done.7.direct_a
  131.3 3.0 %collective-permute-done.12.arrived_b = bf16[528,384]{1,0:T(8,128)(2,1)S(1)} collective-permute-done((bf16[528,384]{1,0:T(8,128)(2,1)S(1)}, bf16[528,384]{1,0:T(8,128)(2,1)S(1)}, u32[]{:S(2)}, u32[]{:S(2)}) %collective-permute-start.12) | collective-permute-done | bytes 405536 | tf_op jit(solution)/shard_map/ppermute | solution.py:631
  134.4 5.6 %collective-permute-done.9.arrived_a = bf16[528,384]{1,0:T(8,128)(2,1)S(1)} collective-permute-done((bf16[528,384]{1,0:T(8,128)(2,1)S(1)}, bf16[528,384]{1,0:T(8,128)(2,1)S(1)}, u32[]{:S(2)}, u32[]{:S(2)}) %collective-permute-start.9) | collective-permute-done | bytes 405536 | tf_op jit(solution)/shard_map/ppermute | solution.py:628
  140.0 1.4 finish.1
  (29 shorter events, 0.2 us)
Async XLA Ops:
  1.8 14.3 %copy-start.4 = (bf16[528,384]{1,0:T(8,128)(2,1)}, bf16[528,384]{1,0:T(8,128)(2,1)S(1)}, u32[]{:S(2)}) copy-start(bf16[528,384]{1,0:T(8,128)(2,1)S(1)} %pad_maximum_fusion.1.own) | copy-start | bytes 1216516
  1.8 12.5 %collective-permute-start = (bf16[528,384]{1,0:T(8,128)(2,1)S(1)}, bf16[528,384]{1,0:T(8,128)(2,1)}, u32[]{:S(2)}, u32[]{:S(2)}) collective-permute-start(bf16[528,384]{1,0:T(8,128)(2,1)S(1)} %pad_maximum_fusion.1.own), channel_id=1, source_target_pairs={{0,1},{1,2},{2,3},{3,0},{4,5},{5,6},{6,7},{7,4},{8,9},{9,10},{10,1... | collective-permute-start | bytes 1216520 | tf_op jit(solution)/shard_map/ppermute | solution.py:628
  4.0 12.1 %collective-permute-start.2 = (bf16[528,384]{1,0:T(8,128)(2,1)S(1)}, bf16[528,384]{1,0:T(8,128)(2,1)}, u32[]{:S(2)}, u32[]{:S(2)}) collective-permute-start(bf16[528,384]{1,0:T(8,128)(2,1)S(1)} %pad_maximum_fusion.1.own), channel_id=1, source_target_pairs={{0,3},{1,0},{2,1},{3,2},{4,7},{5,4},{6,5},{7,6},{8,11},{9,8},{10,9... | collective-permute-start | bytes 1216520 | tf_op jit(solution)/shard_map/ppermute | solution.py:631
  9.0 5.2 %copy-start.14 = (bf16[1024,384]{1,0:T(8,128)(2,1)S(1)}, bf16[1024,384]{1,0:T(8,128)(2,1)}, u32[]{:S(2)}) copy-start(bf16[1024,384]{1,0:T(8,128)(2,1)} %param.12) | copy-start | bytes 2359300
  9.0 7.0 %copy-start.15 = (f32[1536]{0:T(1024)S(1)}, f32[1536]{0:T(1024)}, u32[]{:S(2)}) copy-start(f32[1536]{0:T(1024)} %param.13) | copy-start | bytes 18436
  9.0 7.0 %copy-start = (bf16[1536,384]{1,0:T(8,128)(2,1)S(1)}, bf16[1536,384]{1,0:T(8,128)(2,1)}, u32[]{:S(2)}) copy-start(bf16[1536,384]{1,0:T(8,128)(2,1)} %get-tuple-element.79.o_0.o_1.o_2.others) | copy-start | bytes 3538948
  14.3 27.1 %copy-start.5 = (bf16[512,384]{1,0:T(8,128)(2,1)}, bf16[512,384]{1,0:T(8,128)(2,1)S(1)}, u32[]{:S(2)}) copy-start(bf16[512,384]{1,0:T(8,128)(2,1)S(1)} %slice.11.own) | copy-start | bytes 1179652
  14.3 8.5 %collective-permute-start.1 = (bf16[512,384]{1,0:T(8,128)(2,1)S(1)}, bf16[512,384]{1,0:T(8,128)(2,1)}, u32[]{:S(2)}, u32[]{:S(2)}) collective-permute-start(bf16[512,384]{1,0:T(8,128)(2,1)S(1)} %slice.11.own), channel_id=1, source_target_pairs={{0,3},{1,0},{2,1},{3,2},{4,7},{5,4},{6,5},{7,6},{8,11},{9,8},{10,9... | collective-permute-start | bytes 1179656 | tf_op jit(solution)/shard_map/ppermute | solution.py:631
  15.9 10.5 %collective-permute-start.5 = (bf16[528,384]{1,0:T(8,128)(2,1)}, bf16[528,384]{1,0:T(8,128)(2,1)S(1)}, u32[]{:S(2)}, u32[]{:S(2)}) collective-permute-start(bf16[528,384]{1,0:T(8,128)(2,1)} %collective-permute-done.from_left), channel_id=1, source_target_pairs={{0,1},{1,2},{2,3},{3,0},{4,5},{5,6},{6,7},{7,4},{8,9},{9,10},{10,1... | collective-permute-start | bytes 1216520 | tf_op jit(solution)/shard_map/ppermute | solution.py:628
  16.0 10.4 %copy-start.2 = (bf16[256,768]{1,0:T(8,128)(2,1)S(1)}, bf16[256,768]{1,0:T(8,128)(2,1)}, u32[]{:S(2)}) copy-start(bf16[256,768]{1,0:T(8,128)(2,1)} %get-tuple-element.92.spread) | copy-start | bytes 1179652
  16.0 10.4 %copy-start.9 = (f32[5,1024]{1,0:T(8,128)S(1)}, f32[5,1024]{1,0:T(8,128)}, u32[]{:S(2)}) copy-start(f32[5,1024]{1,0:T(8,128)} %get-tuple-element.89.taps) | copy-start | bytes 61444
  16.1 10.4 %copy-start.10 = (f32[1,128]{1,0:T(1,128)S(1)}, f32[1,128]{1,0:T(1,128)}, u32[]{:S(2)}) copy-start(f32[1,128]{1,0:T(1,128)} %get-tuple-element.94.total) | copy-start | bytes 1540
  16.1 10.4 %copy-start.11 = (f32[1,128]{1,0:T(1,128)S(1)}, f32[1,128]{1,0:T(1,128)}, u32[]{:S(2)}) copy-start(f32[1,128]{1,0:T(1,128)} %get-tuple-element.90.dt_bias) | copy-start | bytes 1540
  22.8 18.6 %collective-permute-start.3 = (bf16[512,384]{1,0:T(8,128)(2,1)S(1)}, bf16[512,384]{1,0:T(8,128)(2,1)}, u32[]{:S(2)}, u32[]{:S(2)}) collective-permute-start(bf16[512,384]{1,0:T(8,128)(2,1)S(1)} %slice.11.own), channel_id=1, source_target_pairs={{0,1},{1,2},{2,3},{3,0},{4,5},{5,6},{6,7},{7,4},{8,9},{9,10},{10,1... | collective-permute-start | bytes 1179656 | tf_op jit(solution)/shard_map/ppermute | solution.py:628
  23.4 23.2 %collective-permute-start.4 = (bf16[512,384]{1,0:T(8,128)(2,1)}, bf16[512,384]{1,0:T(8,128)(2,1)S(1)}, u32[]{:S(2)}, u32[]{:S(2)}) collective-permute-start(bf16[512,384]{1,0:T(8,128)(2,1)} %collective-permute-done.1.from_right), channel_id=1, source_target_pairs={{0,3},{1,0},{2,1},{3,2},{4,7},{5,4},{6,5},{7,6},{8,11},{9,8},{10,9... | collective-permute-start | bytes 1179656 | tf_op jit(solution)/shard_map/ppermute | solution.py:631
  26.4 7.5 %copy-start.3 = (bf16[528,384]{1,0:T(8,128)(2,1)}, bf16[528,384]{1,0:T(8,128)(2,1)S(1)}, u32[]{:S(2)}) copy-start(bf16[528,384]{1,0:T(8,128)(2,1)S(1)} %collective-permute-done.5.piece.rest_2_.far) | copy-start | bytes 1216516
  33.9 12.7 %copy-start.8 = (f32[128,768]{1,0:T(8,128)S(1)}, f32[128,768]{1,0:T(8,128)}, u32[]{:S(2)}) copy-start(f32[128,768]{1,0:T(8,128)} %get-tuple-element.96.rest_0_) | copy-start | bytes 1179652
  33.9 12.6 %collective-permute-start.6 = (bf16[16,1024]{1,0:T(8,128)(2,1)S(1)}, bf16[16,1024]{1,0:T(8,128)(2,1)S(1)}, u32[]{:S(2)}, u32[]{:S(2)}) collective-permute-start(bf16[16,1024]{1,0:T(8,128)(2,1)S(1)} %get-tuple-element.95), channel_id=1, source_target_pairs={{0,4},{4,8},{8,12},{12,16},{16,20},{20,24},{24,28},{28,32},{32,36}... | collective-permute-start | bytes 98312 | tf_op jit(solution)/shard_map/ppermute | solution.py:667
  46.6 7.9 %copy-start.7 = (bf16[512,384]{1,0:T(8,128)(2,1)}, bf16[512,384]{1,0:T(8,128)(2,1)S(1)}, u32[]{:S(2)}) copy-start(bf16[512,384]{1,0:T(8,128)(2,1)S(1)} %collective-permute-done.4.piece.far) | copy-start | bytes 1179652
  54.5 22.7 %all-to-all-start = ((bf16[64,16,128]{2,1,0:T(8,128)(2,1)}), bf16[64,16,128]{2,1,0:T(8,128)(2,1)S(1)}, u32[]{:S(2)}, u32[]{:S(2)}) async-start(bf16[64,16,128]{2,1,0:T(8,128)(2,1)} %get-tuple-element.97), calls=%async_computation | async-start | bytes 524288 | tf_op jit(solution)/shard_map/all_to_all | solution.py:673
  71.3 17.8 %copy-start.16 = (f32[768]{0:T(1024)S(1)}, f32[768]{0:T(1024)}, u32[]{:S(2)}) copy-start(f32[768]{0:T(1024)} %param.22) | copy-start | bytes 9220
  79.3 21.6 %all-to-all-start.1 = ((bf16[64,16,128]{2,1,0:T(8,128)(2,1)}), bf16[64,16,128]{2,1,0:T(8,128)(2,1)}, u32[]{:S(2)}, u32[]{:S(2)}) async-start(bf16[64,16,128]{2,1,0:T(8,128)(2,1)} %scan.1), calls=%async_computation.1 | async-start | bytes 524288 | tf_op jit(solution)/shard_map/all_to_all | solution.py:686
  93.0 7.9 %copy-start.1 = (f32[1024,128]{1,0:T(8,128)S(1)}, f32[1024,128]{1,0:T(8,128)}, u32[]{:S(2)}) copy-start(f32[1024,128]{1,0:T(8,128)} %get-tuple-element.100.decay) | copy-start | bytes 1572868
  101.0 5.5 %copy-start.6 = (f32[128,768]{1,0:T(8,128)S(1)}, f32[128,768]{1,0:T(8,128)}, u32[]{:S(2)}) copy-start(f32[128,768]{1,0:T(8,128)} %get-tuple-element.111.earlier) | copy-start | bytes 1179652
  105.7 12.6 %collective-permute-start.11 = (bf16[528,384]{1,0:T(8,128)(2,1)}, bf16[528,384]{1,0:T(8,128)(2,1)S(1)}, u32[]{:S(2)}, u32[]{:S(2)}) collective-permute-start(bf16[528,384]{1,0:T(8,128)(2,1)} %get-tuple-element.126), channel_id=1, source_target_pairs={{0,3},{1,0},{2,1},{3,2},{4,7},{5,4},{6,5},{7,6},{8,11},{9,8},{10,9... | collective-permute-start | bytes 1216520 | tf_op jit(solution)/shard_map/ppermute | solution.py:631
  106.5 5.3 %copy-start.12 = (bf16[528,768]{1,0:T(8,128)(2,1)S(1)}, bf16[528,768]{1,0:T(8,128)(2,1)}, u32[]{:S(2)}) copy-start(bf16[528,768]{1,0:T(8,128)(2,1)} %get-tuple-element.113.scaled_b) | copy-start | bytes 2433028
  111.0 11.6 %collective-permute-start.8 = (bf16[528,384]{1,0:T(8,128)(2,1)}, bf16[528,384]{1,0:T(8,128)(2,1)S(1)}, u32[]{:S(2)}, u32[]{:S(2)}) collective-permute-start(bf16[528,384]{1,0:T(8,128)(2,1)} %get-tuple-element.122), channel_id=1, source_target_pairs={{0,1},{1,2},{2,3},{3,0},{4,5},{5,6},{6,7},{7,4},{8,9},{9,10},{10,1... | collective-permute-start | bytes 1216520 | tf_op jit(solution)/shard_map/ppermute | solution.py:628
  111.8 1.1 copy-start.13
  115.5 15.8 %collective-permute-start.10 = (bf16[528,384]{1,0:T(8,128)(2,1)S(1)}, bf16[528,384]{1,0:T(8,128)(2,1)S(1)}, u32[]{:S(2)}, u32[]{:S(2)}) collective-permute-start(bf16[528,384]{1,0:T(8,128)(2,1)S(1)} %get-tuple-element.124), channel_id=1, source_target_pairs={{0,1},{1,2},{2,3},{3,0},{4,5},{5,6},{6,7},{7,4},{8,9},{9,10},{10,1... | collective-permute-start | bytes 1216520 | tf_op jit(solution)/shard_map/ppermute | solution.py:628
  115.6 15.7 %collective-permute-start.7 = (bf16[528,384]{1,0:T(8,128)(2,1)S(1)}, bf16[528,384]{1,0:T(8,128)(2,1)S(1)}, u32[]{:S(2)}, u32[]{:S(2)}) collective-permute-start(bf16[528,384]{1,0:T(8,128)(2,1)S(1)} %get-tuple-element.120), channel_id=1, source_target_pairs={{0,3},{1,0},{2,1},{3,2},{4,7},{5,4},{6,5},{7,6},{8,11},{9,8},{10,9... | collective-permute-start | bytes 1216520 | tf_op jit(solution)/shard_map/ppermute | solution.py:631
  118.4 16.0 %collective-permute-start.12 = (bf16[528,384]{1,0:T(8,128)(2,1)S(1)}, bf16[528,384]{1,0:T(8,128)(2,1)S(1)}, u32[]{:S(2)}, u32[]{:S(2)}) collective-permute-start(bf16[528,384]{1,0:T(8,128)(2,1)S(1)} %add.44), channel_id=1, source_target_pairs={{0,3},{1,0},{2,1},{3,2},{4,7},{5,4},{6,5},{7,6},{8,11},{9,8},{10,9... | collective-permute-start | bytes 1216520 | tf_op jit(solution)/shard_map/ppermute | solution.py:631
  122.7 17.3 %collective-permute-start.9 = (bf16[528,384]{1,0:T(8,128)(2,1)S(1)}, bf16[528,384]{1,0:T(8,128)(2,1)S(1)}, u32[]{:S(2)}, u32[]{:S(2)}) collective-permute-start(bf16[528,384]{1,0:T(8,128)(2,1)S(1)} %add.43), channel_id=1, source_target_pairs={{0,1},{1,2},{2,3},{3,0},{4,5},{5,6},{6,7},{7,4},{8,9},{9,10},{10,1... | collective-permute-start | bytes 1216520 | tf_op jit(solution)/shard_map/ppermute | solution.py:628
